TPU v7x, 512 devices: a whole 4x4x16 slice. The times are simulated.
512 devices in a mesh: seq: 64 (over z, x), tp: 8 (over y, core).
Axes of the slice: x: 4, y: 4, z: 16, core: 2. Of those that a mesh axis runs over, the one named last changes fastest.
Arguments:
- prefill_hidden: bfloat16 [8192, 5120], P('seq', 'tp'), may hold values from -14 to 14
- prefill_query_rows: bfloat16 [8192, 5120], P('seq', 'tp'), may hold values from -250 to 250
- prefill_key_value: bfloat16 [2, 8192, 1024], P(None, 'seq', 'tp'), may hold values from -5 to 5
- request_prefix_cache: bfloat16 [2, 64, 768, 1024], P(None, 'seq', None, 'tp'), may hold values from -5 to 5
- prefix_lengths: int32 [64], replicated, may hold values from 0 to 768, as said below
- decode_hidden: bfloat16 [4, 5120], P(None, 'tp'), may hold values from -14 to 14
- decode_query_rows: bfloat16 [4, 5120], P(None, 'tp'), may hold values from -250 to 250
- decode_kv: bfloat16 [2, 4, 1024], P(None, None, 'tp'), may hold values from -5 to 5
- decode_slot_cache: bfloat16 [2, 5, 8192, 1024], P(None, None, 'seq', 'tp'), may hold values from -5 to 5
- cache_lengths: int32 [4], replicated, may hold values from 2048 to 8192, as said below
- slot_table: int32 [4], replicated, may hold values from 0 to 4, as said below
- out_weight: bfloat16 [5120, 5120], P('tp', 'seq'), may hold values from -0.078125 to 0.078125
- final_gain: bfloat16 [5120], replicated, may hold values from 0.5 to 1.5
- head_weight: bfloat16 [5120, 152064], P(None, ('seq', 'tp')), may hold values from -4 to 4
Outputs:
- prefill_out: bfloat16 [8192, 5120], P('seq', 'tp')
- decode_out: bfloat16 [4, 5120], P(None, 'tp')
- log_probs: float32 [68, 152064], P(None, ('seq', 'tp'))
Inputs may be any that keep to these rules, and one draw needn't show every extreme that they name: `prefix_lengths`: some request has no cached prefix and some has exactly 768 cached tokens. `cache_lengths`: some request has exactly 8192 cached tokens. `slot_table`: distinct slots.
All inputs are finite; a program needn't handle non-finite values.
Results may differ from a plain program's by a relative error of at most 0.0035.
Values may be sent and summed in bfloat16 or wider, within the bound.
A program may use at most 128 MiB of HBM per device.

v0:
```python
import math

import jax
import jax.numpy as jnp
from jax import lax
from jax.sharding import PartitionSpec as P

QUERY_HEADS = 40
KEY_HEADS = 8
HEAD_SIZE = 128


neg_large = -1e30
exact = lax.Precision.HIGHEST
norm_eps = 1e-06


def merged(value, axis, join):
    pieces = jax.tree.map(lambda part: lax.all_gather(part, axis), value)
    head = jax.tree.map(lambda part: part[0], pieces)
    tail = jax.tree.map(lambda part: part[1:], pieces)
    subtotal, _ = lax.scan(lambda subtotal, piece: (join(subtotal, piece), None), head, tail)
    return subtotal


def join_parts(earlier, later):
    row_max = jnp.maximum(earlier[0], later[0])
    factor_one = jnp.exp(earlier[0] - row_max)
    factor_two = jnp.exp(later[0] - row_max)
    return (
        row_max,
        earlier[1] * factor_one + later[1] * factor_two,
        earlier[2] * factor_one[..., None] + later[2] * factor_two[..., None],
    )


def join_totals(earlier, later):
    row_max = jnp.maximum(earlier[0], later[0])
    return (
        row_max,
        earlier[1] * jnp.exp(earlier[0] - row_max) + later[1] * jnp.exp(later[0] - row_max),
    )


def local(
    prefill_hidden,
    prefill_query_rows,
    prefill_key_value,
    request_prefix_cache,
    prefix_lengths,
    decode_hidden,
    decode_query_rows,
    decode_kv,
    decode_slot_cache,
    cache_lengths,
    slot_table,
    out_weight,
    final_gain,
    head_weight,
):
    query_group_width = QUERY_HEADS // KEY_HEADS
    score_scale = 1.0 / math.sqrt(HEAD_SIZE)
    kv_local = prefill_key_value.shape[2] // HEAD_SIZE
    seq_index = lax.axis_index("seq")
    span_len = prefill_query_rows.shape[0]
    prefix_len = request_prefix_cache.shape[2]
    prefix_end = lax.dynamic_slice_in_dim(prefix_lengths, seq_index, 1)[0]
    query_matrix = prefill_query_rows.reshape(span_len, kv_local, query_group_width, HEAD_SIZE)
    joined_keys = jnp.concatenate([request_prefix_cache[0, 0], prefill_key_value[0]], 0).reshape(
        prefix_len + span_len, kv_local, HEAD_SIZE
    )
    value_matrix = jnp.concatenate([request_prefix_cache[1, 0], prefill_key_value[1]], 0).reshape(
        prefix_len + span_len, kv_local, HEAD_SIZE
    )
    key_place = jnp.arange(prefix_len + span_len)
    query_place = jnp.arange(span_len)
    live_mask = jnp.where(
        key_place[None, :] < prefix_len,
        key_place[None, :] < prefix_end,
        key_place[None, :] - prefix_len <= query_place[:, None],
    )
    scores = (
        jnp.einsum("rkgh,skh->kgrs", query_matrix, joined_keys, preferred_element_type=jnp.float32)
        * score_scale
    )
    masked = jnp.where(live_mask, scores, neg_large)
    row_max = jnp.max(masked, axis=-1, keepdims=True)
    weights = jnp.where(live_mask, jnp.exp(masked - row_max), 0.0)
    row_sum = jnp.sum(weights, axis=-1)
    weights_low = weights.astype(jnp.bfloat16)
    mixed = jnp.einsum(
        "kgrs,skh->rkgh", weights_low, value_matrix, preferred_element_type=jnp.float32
    )
    prefill_attention = (
        (mixed / jnp.transpose(row_sum, (2, 0, 1))[..., None])
        .astype(jnp.bfloat16)
        .reshape(span_len, -1)
    )
    decode_count = decode_query_rows.shape[0]
    ctx_local = decode_slot_cache.shape[2]
    chosen = jnp.take(decode_slot_cache, slot_table, axis=1)
    positions = seq_index * ctx_local + jnp.arange(ctx_local)
    decode_live = (positions[None, :] < cache_lengths[:, None])[:, None, None, :]
    decode_token_rows = decode_query_rows.reshape(
        decode_count, kv_local, query_group_width, HEAD_SIZE
    )
    cache_keys = chosen[0].reshape(decode_count, ctx_local, kv_local, HEAD_SIZE)
    cache_values = chosen[1].reshape(decode_count, ctx_local, kv_local, HEAD_SIZE)
    decode_scores = (
        jnp.einsum(
            "bkgh,bskh->bkgs", decode_token_rows, cache_keys, preferred_element_type=jnp.float32
        )
        * score_scale
    )
    decode_masked = jnp.where(decode_live, decode_scores, neg_large)
    decode_max = jnp.max(decode_masked, axis=-1)
    decode_weights = jnp.where(decode_live, jnp.exp(decode_masked - decode_max[..., None]), 0.0)
    decode_sum = jnp.sum(decode_weights, axis=-1)
    decode_mixed = jnp.einsum(
        "bkgs,bskh->bkgh", decode_weights, cache_values.astype(jnp.float32), precision=exact
    )
    best = lax.pmax(decode_max, "seq")
    factors = jnp.exp(decode_max - best)
    totals, mixtures = lax.psum((decode_sum * factors, decode_mixed * factors[..., None]), "seq")
    combined = (best, totals, mixtures)
    own_keys = decode_kv[0].reshape(decode_count, kv_local, HEAD_SIZE)
    own_values = decode_kv[1].reshape(decode_count, kv_local, HEAD_SIZE).astype(jnp.float32)
    own_scores = (
        jnp.einsum("bkgh,bkh->bkg", decode_token_rows, own_keys, preferred_element_type=jnp.float32)
        * score_scale
    )
    own_mixed = jnp.broadcast_to(own_values[:, :, None, :], combined[2].shape)
    final_max, final_sum, final_mixed = join_parts(
        combined, (own_scores, jnp.ones_like(own_scores), own_mixed)
    )
    decode_attention = (
        (final_mixed / final_sum[..., None]).astype(jnp.bfloat16).reshape(decode_count, -1)
    )
    attention_all = jnp.concatenate([prefill_attention, decode_attention], 0)
    every_row = lax.all_gather(attention_all, "seq", axis=0, tiled=True)
    column_block = jnp.dot(every_row, out_weight, preferred_element_type=jnp.float32)
    partial_terms = lax.all_to_all(column_block, "seq", split_axis=0, concat_axis=1, tiled=True)
    summed = lax.psum_scatter(partial_terms, "tp", scatter_dimension=1, tiled=True)
    residual = jnp.concatenate([prefill_hidden, decode_hidden], 0).astype(jnp.float32)
    updated = (residual + summed).astype(jnp.bfloat16)
    prefill_out = updated[:span_len]
    decode_out = updated[span_len:]
    gathered = lax.all_gather(prefill_out[span_len - 1 :], ("seq", "tp"), axis=0, tiled=True)
    decode_full = lax.all_gather(decode_out, "tp", axis=1, tiled=True)
    n_seq = lax.axis_size("seq")
    n_tp = lax.axis_size("tp")
    feature_width = prefill_out.shape[1]
    prefill_full = gathered.reshape(n_seq, n_tp * feature_width)
    head_input = jnp.concatenate([decode_full, prefill_full], 0).astype(jnp.float32)
    mean_square = jnp.mean(head_input * head_input, axis=-1, keepdims=True)
    normed = (
        head_input * lax.rsqrt(mean_square + norm_eps) * final_gain.astype(jnp.float32)
    ).astype(jnp.bfloat16)
    logits = jnp.dot(normed, head_weight, preferred_element_type=jnp.float32)
    local_max = jnp.max(logits, axis=-1)
    local_sum = jnp.sum(jnp.exp(logits - local_max[:, None]), axis=-1)
    global_max, global_sum = merged((local_max, local_sum), ("seq", "tp"), join_totals)
    log_probs = logits - (global_max + jnp.log(global_sum))[:, None]
    return (prefill_out, decode_out, log_probs)


def solution(mesh):
    return jax.shard_map(
        local,
        mesh=mesh,
        in_specs=(
            P("seq", "tp"),
            P("seq", "tp"),
            P(None, "seq", "tp"),
            P(None, "seq", None, "tp"),
            P(),
            P(None, "tp"),
            P(None, "tp"),
            P(None, None, "tp"),
            P(None, None, "seq", "tp"),
            P(),
            P(),
            P("tp", "seq"),
            P(),
            P(None, ("seq", "tp")),
        ),
        out_specs=(P("seq", "tp"), P(None, "tp"), P(None, ("seq", "tp"))),
        check_vma=False,
    )
```

profile of v0, /device:TPU:1, one launch (start us, length us, event | category | flops | bytes accessed | tf_op | source)
XLA Modules:
  0.0 1924.1 jit_solution(15863495507919026672)
XLA Ops:
  7.2 1.3 compare_select_fusion
  8.6 1.2 compare_and_fusion
  9.8 1.2 dynamic_slice.10
  11.7 1.7 fusion.58
  13.4 1.4 fusion.59
  14.8 1.7 copy.40
  17.6 1.5 fusion.5
  21.4 1.2 broadcast_compare_fusion
  22.6 1.6 gather_fusion
  27.4 122.6 %pmax.7 = f32[4,1,5]{2,0,1:T(4,128)S(1)} all-reduce(f32[4,1,5]{2,0,1:T(4,128)S(1)} %bitcast.143), channel_id=1, replica_groups=mesh['seq'=64,'tp'=8] {'seq'}, use_global_device_ids=true, to_apply=%region_3.4 | all-reduce | flops 20 | bytes 160 | tf_op jit(solution)/shard_map/pmax | solution.py:122
  150.0 1.2 fusion.24
  151.3 219.7 %all-reduce.3 = (f32[4,1,5]{2,0,1:T(4,128)S(1)}, f32[4,1,5,128]{3,2,0,1:T(8,128)S(1)}) all-reduce(f32[4,1,5]{2,0,1:T(4,128)S(1)} %get-tuple-element.57, f32[4,1,5,128]{3,2,0,1:T(8,128)S(1)} %fusion.24), channel_id=1, replica_groups=mesh['seq'=64,'tp'=8] {'seq'}, use_global_device_ids=true, to_apply=%region_6.7 | all-reduce | flops 2580 | bytes 20640 | tf_op jit(solution)/shard_map/psum | solution.py:124
  371.9 235.7 %all-gather.6.cloned.1.call-done = bf16[64,132,640]{2,1,0:T(8,128)(2,1)} async-done(((bf16[1,132,640]{2,1,0:T(8,128)(2,1)}), bf16[64,132,640]{2,1,0:T(8,128)(2,1)}) %all-gather.6.cloned.1.call-update) | async-done | bytes 10813456 | tf_op jit(solution)/shard_map/all_gather | solution.py:140
  607.6 13.8 reshape.202
  621.4 8.7 fusion.62
  630.1 8.9 all_to_all.14
  639.0 6.4 copy.45
  645.4 205.2 %all_to_all.19 = f32[64,132,80]{2,1,0:T(8,128)S(1)} all-to-all(f32[64,132,80]{2,1,0:T(8,128)} %copy.45), channel_id=1, replica_groups=mesh['seq'=64,'tp'=8] {'seq'}, dimensions={0} | all-to-all | bytes 5406720 | tf_op jit(solution)/shard_map/all_to_all | solution.py:142
  850.6 2.8 copy.46
  853.4 5.6 all_to_all.17
  860.3 37.6 %reduce-scatter.2.cloned.1.call-done = f32[132,640]{1,0:T(8,128)} async-done(((f32[132,5120]{1,0:T(8,128)}), f32[132,640]{1,0:T(8,128)}) %reduce-scatter.2.cloned.1.call-update) | async-done | bytes 337936 | tf_op jit(solution)/shard_map/reduce_scatter | solution.py:143
  899.0 163.8 %all-gather.3 = bf16[512,1,640]{2,1,0:T(2,128)(2,1)} all-gather(bf16[1,1,640]{2,1,0:T(2,128)(2,1)S(1)} %slice_bitcast_fusion.6), channel_id=1, replica_groups=mesh['seq'=64,'tp'=8] {'seq','tp'}, dimensions={0}, use_global_device_ids=true | all-gather | bytes 656640 | tf_op jit(solution)/shard_map/all_gather | solution.py:148
  1062.8 5.8 reduce.6
  1068.6 2.2 reshape.178
  1070.8 12.8 all_gather.22
  1083.5 1.4 fusion.8
  1085.0 2.3 fusion.61
  1088.2 1.4 dynamic-update-slice
  1091.3 449.4 %all-reduce.6.cloned.1.call-done = (f32[34816]{0:T(1024)}, f32[34816]{0:T(1024)}) async-done(((f32[34816]{0:T(1024)}, f32[34816]{0:T(1024)}), (f32[34816]{0:T(1024)}, f32[34816]{0:T(1024)})) %all-reduce.6.cloned.1.call-update) | async-done | bytes 278544
  1544.1 1.1 reshape.195
  1545.2 1.1 reshape.196
  1546.2 370.6 %while.12 = (s32[]{:T(128)}, f32[68]{0:T(128)S(1)}, f32[68]{0:T(128)S(1)}, f32[511,68]{1,0:T(8,128)}, f32[511,68]{1,0:T(8,128)}, /*index=5*/s32[]{:T(128)}) while((s32[]{:T(128)}, f32[68]{0:T(128)S(1)}, f32[68]{0:T(128)S(1)}, f32[511,68]{1,0:T(8,128)}, f32[511,68]{1,0:T(8,128)}, /*index=5*/s32[]{:T(128)}) %tuple.35), condition=%wide.region_12.13_spmd, body=%wide.region_11.12_spmd.sunk | while | flops 410 | bytes 1705 | solution.py:22
  (576 shorter events, 383.6 us)
Async XLA Ops:
  7.2 1077.8 %copy-start = (bf16[5120,297]{0,1:T(8,128)(2,1)S(1)}, bf16[5120,297]{0,1:T(8,128)(2,1)}, u32[]{:S(2)}) copy-start(bf16[5120,297]{0,1:T(8,128)(2,1)} %param.29) | copy-start | bytes 9123844
  7.2 600.5 %all-gather.6.cloned.1.call-start = ((), (), s32[]{:S(2)}) async-start(), calls=%async_computation.3 | async-start | bytes 11315200 | tf_op jit(solution)/shard_map/all_gather | solution.py:140
  19.7 0.9 copy-start.10
  19.7 131.5 %copy-start.9 = (bf16[2,4,128]{2,1,0:T(4,128)(2,1)S(1)}, bf16[2,4,128]{2,1,0:T(4,128)(2,1)}, u32[]{:S(2)}) copy-start(bf16[2,4,128]{2,1,0:T(4,128)(2,1)} %param.23) | copy-start | bytes 6148
  24.9 0.7 copy-start.2
  371.9 249.5 %copy-start.4 = (bf16[640,80]{0,1:T(8,128)(2,1)S(1)}, bf16[640,80]{0,1:T(8,128)(2,1)}, u32[]{:S(2)}) copy-start(bf16[640,80]{0,1:T(8,128)(2,1)} %param.27) | copy-start | bytes 307204
  371.9 526.0 %reduce-scatter.2.cloned.1.call-start = ((), (), s32[]{:S(2)}) async-start(), calls=%async_computation.2 | async-start | bytes 3133440 | tf_op jit(solution)/shard_map/reduce_scatter | solution.py:143
  859.0 0.7 copy-start.7
  859.0 38.9 %copy-start.3 = (bf16[128,640]{1,0:T(8,128)(2,1)S(1)}, bf16[128,640]{1,0:T(8,128)(2,1)}, u32[]{:S(2)}) copy-start(bf16[128,640]{1,0:T(8,128)(2,1)} %param.16) | copy-start | bytes 491524
  859.0 38.9 %copy-start.8 = (bf16[4,640]{1,0:T(4,128)(2,1)S(1)}, bf16[4,640]{1,0:T(4,128)(2,1)}, u32[]{:S(2)}) copy-start(bf16[4,640]{1,0:T(4,128)(2,1)} %param.21) | copy-start | bytes 15364
  859.0 681.7 %all-reduce.6.cloned.1.call-start = ((), (), s32[]{:S(2)}) async-start(), calls=%async_computation.4 | async-start | bytes 557056
  898.9 171.8 %copy-start.6 = (bf16[4,640]{1,0:T(4,128)(2,1)}, bf16[4,640]{1,0:T(4,128)(2,1)S(1)}, u32[]{:S(2)}) copy-start(bf16[4,640]{1,0:T(4,128)(2,1)S(1)} %slice.70) | copy-start | bytes 15364
  1062.8 22.2 %copy-start.5 = (f32[5120]{0:T(1024)S(1)}, f32[5120]{0:T(1024)}, u32[]{:S(2)}) copy-start(f32[5120]{0:T(1024)} %convert_element_type.45) | copy-start | bytes 61444
  1089.9 0.7 copy-start.1
Sparse Core Ops, SparseCore 0:
  372.0 235.5 all-gather.5
  859.1 38.7 reduce-scatter.1
  1090.7 449.9 all-reduce.5
where the time goes:
time: 1960 us; the launch traced here: 1920 us
  blocking collectives  724 us (37%)
  waiting for transfers between devices  723 us (37%)
  other arithmetic  385 us (20%)
  local copies, waits for them, and re-layouts  59 us (3%)
    unnamed x4, waiting for transfers between devices  449 us
    add x511, other arithmetic, join_totals(): earlier[1] * jnp.exp(earlier[0] - row_max)  366 us
    all_gather x1, waiting for transfers between devices, local(): every_row = lax.all_gather(attention_all, 'seq', axis=0, tiled=True)  236 us
    psum x1, blocking collectives, local(): lax.psum((decode_sum * factors, decode_mixed * factors[..., None]), 'seq')  220 us
    all_to_all x1, blocking collectives, local(): lax.all_to_all(column_block, 'seq', split_axis=0, concat_axis=1, tiled=True)  205 us
    all_gather x1, blocking collectives, local(): lax.all_gather(prefill_out[span_len - 1:], ('seq', 'tp'), axis=0, tiled=T...  164 us
    pmax x1, blocking collectives, local(): best = lax.pmax(decode_max, 'seq')  123 us
  transfers between devices with their start and end apart: 3, of which 3 were waited for; matrix products, arithmetic and copies ran while one was open for 0% of the time, Pallas kernels for 0%

commit v1 on v0

v1 whole, which is shorter than its diff:
```python
import math

import jax
import jax.numpy as jnp
from jax import lax
from jax.experimental import pallas as pl
from jax.experimental.pallas import tpu as pltpu
from jax.sharding import PartitionSpec as P

NEG = -1e30
EPS = 1e-6
NT = (((1,), (1,)), ((), ()))
MESH = pl.DeviceIdType.MESH
F32 = jnp.float32
BF16 = jnp.bfloat16

NX, NY, NZ, NC = 4, 4, 16, 2
WC = 80
HD = 128
GROUP = 5
KW = 640


def fori(lo, hi, body):
    def step(i, carry):
        body(i)
        return carry

    lax.fori_loop(lo, hi, step, 0)


def mod(a, n):
    return lax.rem(a + n, n)


def kernel(
    prefix_len_ref,
    cache_len_ref,
    slot_ref,
    hid_ref,
    q_ref,
    kv_ref,
    pre_ref,
    dhid_ref,
    dq_ref,
    dkv_ref,
    dcache_ref,
    w_ref,
    gain_ref,
    hw_ref,
    out_ref,
    dout_ref,
    lp_ref,
    hwbuf,
    wbuf,
    abuf,
    qd,
    dpart,
    dxb,
    dz1,
    dz2,
    dfin,
    dmat,
    cs_main,
    cs_dec,
    cr_main,
    cr_dec,
    co_main,
    co_dec,
    msg,
    rbuf,
    big,
    agz,
    hbuf,
    tmat,
    lst,
    lsz,
    hw_sem,
    wr_s,
    wr_r,
    wl_s,
    wl_r,
    a_s,
    a_r,
    dx_s,
    dx_r,
    d1_s,
    d1_r,
    d2_s,
    d2_r,
    df_s,
    df_r,
    cm_s,
    cm_r,
    cd_s,
    cd_r,
    r_s,
    r_r,
    gz_s,
    gz_r,
    hb_s,
    hb_r,
    hc_s,
    hc_r,
    db_s,
    db_r,
    dc_s,
    dc_r,
    ls_s,
    ls_r,
    lz_s,
    lz_r,
):
    s = lax.axis_index("seq")
    t = lax.axis_index("tp")
    z, x = lax.div(s, NX), lax.rem(s, NX)
    y, c = lax.div(t, NC), lax.rem(t, NC)
    scale = 1.0 / math.sqrt(HD)

    def dev(zz, xx, yy, cc):
        return (zz * NX + xx, yy * NC + cc)

    def rcopy(src, dst, ss, rs, device):
        return pltpu.make_async_remote_copy(
            src_ref=src, dst_ref=dst, send_sem=ss, recv_sem=rs, device_id=device, device_id_type=MESH
        )

    hw_copy = pltpu.make_async_copy(hw_ref, hwbuf, hw_sem)
    hw_copy.start()

    barrier = pltpu.get_barrier_semaphore()

    def plane(p):
        q = lax.rem(x * 8 + t + p, 32)
        return (z * NX + lax.div(q, 8), lax.rem(q, 8))

    def sig_z(d):
        pl.semaphore_signal(barrier, inc=1, device_id=dev(mod(z + d, NZ), x, y, c), device_id_type=MESH)

    def sig_p(p):
        pl.semaphore_signal(barrier, inc=1, device_id=plane(p), device_id_type=MESH)

    fori(1, NZ, sig_z)
    fori(1, 32, sig_p)

    eye = (
        lax.broadcasted_iota(jnp.int32, (WC, WC), 0) == lax.broadcasted_iota(jnp.int32, (WC, WC), 1)
    ).astype(F32).astype(BF16)
    wbuf[z] = lax.dot_general(eye, w_ref[...], NT, preferred_element_type=F32).astype(BF16)

    qd[...] = jnp.zeros_like(qd)
    dq = dq_ref[...].astype(F32)
    for r in range(4):
        for h in range(GROUP):
            qd[r * 8 + h : r * 8 + h + 1, :] = dq[r : r + 1, h * HD : (h + 1) * HD]
    qall = qd[...].astype(BF16)
    row = lax.broadcasted_iota(jnp.int32, (32, 1), 0)
    rows_slot = jnp.zeros((32, 1), jnp.int32)
    rows_len = jnp.zeros((32, 1), jnp.int32)
    for r in range(4):
        inside = lax.div(row, 8) == r
        rows_slot = jnp.where(inside, slot_ref[r], rows_slot)
        rows_len = jnp.where(inside, cache_len_ref[r], rows_len)
    keys = dcache_ref[0].reshape(5 * 128, HD)
    vals = dcache_ref[1].reshape(5 * 128, HD)
    col = lax.broadcasted_iota(jnp.int32, (32, 640), 1)
    live = (lax.div(col, 128) == rows_slot) & (s * 128 + lax.rem(col, 128) < rows_len)
    sc = lax.dot_general(qall, keys, NT, preferred_element_type=F32) * scale
    sc = jnp.where(live, sc, NEG)
    dm = jnp.max(sc, axis=-1, keepdims=True)
    dw = jnp.where(live, jnp.exp(sc - dm), 0.0)
    dl = jnp.sum(dw, axis=-1, keepdims=True)
    hi = dw.astype(BF16)
    lo = (dw - hi.astype(F32)).astype(BF16)
    do = jnp.dot(hi, vals, preferred_element_type=F32) + jnp.dot(lo, vals, preferred_element_type=F32)
    lane = lax.broadcasted_iota(jnp.int32, (32, HD), 1)
    dstat = jnp.where(lane < 64, dm, dl)
    for r in range(4):
        dpart[r, 0:8, :] = do[r * 8 : r * 8 + 8]
        dpart[r, 8:16, :] = dstat[r * 8 : r * 8 + 8]

    pl.semaphore_wait(barrier, NZ - 1 + 31)

    def w_right(k):
        b = mod(z - k + 1, NZ)
        return rcopy(wbuf.at[b], wbuf.at[b], wr_s.at[k], wr_r.at[k], dev(mod(z + 1, NZ), x, y, c))

    def w_left(k):
        b = mod(z + k - 1, NZ)
        return rcopy(wbuf.at[b], wbuf.at[b], wl_s.at[k], wl_r.at[k], dev(mod(z - 1, NZ), x, y, c))

    def w_right_in(k):
        b = mod(z - k, NZ)
        return rcopy(wbuf.at[b], wbuf.at[b], wr_s.at[k], wr_r.at[k], dev(mod(z + 1, NZ), x, y, c))

    def w_left_in(k):
        b = mod(z + k, NZ)
        return rcopy(wbuf.at[b], wbuf.at[b], wl_s.at[k], wl_r.at[k], dev(mod(z - 1, NZ), x, y, c))

    def w_forward(k):
        w_right_in(k).wait_recv()
        if k < 8:
            w_right(k + 1).start()
        if k < 8:
            w_left_in(k).wait_recv()
            if k < 7:
                w_left(k + 1).start()

    w_right(1).start()
    w_left(1).start()

    def dx(d):
        xx = mod(x + d, NX)
        return rcopy(dpart.at[xx], dxb.at[x], dx_s.at[d], dx_r.at[d], dev(z, xx, y, c))

    dxb[x] = dpart[x]
    fori(1, NX, lambda d: dx(d).start())

    pe = prefix_len_ref[s]
    kp, ko = pre_ref[0, 0], kv_ref[0]
    vp, vo = pre_ref[1, 0], kv_ref[1]
    n_pre = kp.shape[0]
    live1 = lax.broadcasted_iota(jnp.int32, (128, n_pre), 1) < pe
    live2 = lax.broadcasted_iota(jnp.int32, (128, 128), 1) <= lax.broadcasted_iota(jnp.int32, (128, 128), 0)

    def head(h):
        hs = pl.ds(pl.multiple_of(h * HD, HD), HD)
        qh = q_ref[:, hs]
        s1 = lax.dot_general(qh, kp, NT, preferred_element_type=F32) * scale
        s2 = lax.dot_general(qh, ko, NT, preferred_element_type=F32) * scale
        s1 = jnp.where(live1, s1, NEG)
        s2 = jnp.where(live2, s2, NEG)
        m = jnp.maximum(jnp.max(s1, -1, keepdims=True), jnp.max(s2, -1, keepdims=True))
        p1 = jnp.where(live1, jnp.exp(s1 - m), 0.0)
        p2 = jnp.where(live2, jnp.exp(s2 - m), 0.0)
        total = jnp.sum(p1, -1, keepdims=True) + jnp.sum(p2, -1, keepdims=True)
        o = jnp.dot(p1.astype(BF16), vp, preferred_element_type=F32)
        o += jnp.dot(p2.astype(BF16), vo, preferred_element_type=F32)
        abuf[x, :, hs] = (o / total).astype(BF16)

    fori(0, GROUP, head)
    w_forward(1)

    def a_copy(d, src):
        return rcopy(abuf.at[src], abuf.at[src], a_s.at[d], a_r.at[d], dev(z, mod(x + d, NX), y, c))

    fori(1, NX, lambda d: a_copy(d, x).start())

    def merge(ref):
        os = [ref[i, 0:8, :] for i in range(4)]
        st = [ref[i, 8:16, :] for i in range(4)]
        ms = [a[:, 0:1] for a in st]
        lls = [a[:, 64:65] for a in st]
        m = jnp.maximum(jnp.maximum(ms[0], ms[1]), jnp.maximum(ms[2], ms[3]))
        o, l = 0.0, 0.0
        for i in range(4):
            f = jnp.exp(ms[i] - m)
            o = o + os[i] * f
            l = l + lls[i] * f
        return o, m, l

    lane8 = lax.broadcasted_iota(jnp.int32, (8, HD), 1)

    def dx_in(d):
        return rcopy(dpart.at[x], dxb.at[mod(x - d, NX)], dx_s.at[d], dx_r.at[d], dev(z, mod(x + d, NX), y, c))

    fori(1, NX, lambda d: dx_in(d).wait_recv())
    o, m, l = merge(dxb)
    zl, zg = lax.rem(z, 4), lax.div(z, 4)
    dz1[zl, 0:8, :] = o
    dz1[zl, 8:16, :] = jnp.where(lane8 < 64, m, l)

    def d1(d, slot):
        return rcopy(dz1.at[slot], dz1.at[slot], d1_s.at[d], d1_r.at[d], dev(zg * 4 + mod(zl + d, 4), x, y, c))

    fori(1, 4, lambda d: d1(d, zl).start())
    w_forward(2)
    fori(1, 4, lambda d: d1(d, mod(zl - d, 4)).wait_recv())
    o, m, l = merge(dz1)
    dz2[zg, 0:8, :] = o
    dz2[zg, 8:16, :] = jnp.where(lane8 < 64, m, l)

    def d2(d, slot):
        return rcopy(dz2.at[slot], dz2.at[slot], d2_s.at[d], d2_r.at[d], dev(mod(zg + d, 4) * 4 + zl, x, y, c))

    fori(1, 4, lambda d: d2(d, zg).start())
    w_forward(3)
    fori(1, 4, lambda d: d2(d, mod(zg - d, 4)).wait_recv())
    o, m, l = merge(dz2)
    row4 = lax.broadcasted_iota(jnp.int32, (4, HD), 0)
    own_k = jnp.sum(jnp.where(row4 == x, dkv_ref[0].astype(F32), 0.0), axis=0, keepdims=True)
    own_v = jnp.sum(jnp.where(row4 == x, dkv_ref[1].astype(F32), 0.0), axis=0, keepdims=True)
    own_q = qd[pl.ds(pl.multiple_of(x * 8, 8), 8), :]
    own_s = jnp.sum(own_q * own_k, axis=-1, keepdims=True) * scale
    m2 = jnp.maximum(m, own_s)
    f1, f2 = jnp.exp(m - m2), jnp.exp(own_s - m2)
    dfin[x] = (o * f1 + own_v * f2) / (l * f1 + f2)

    def df(d, slot):
        return rcopy(dfin.at[slot], dfin.at[slot], df_s.at[d], df_r.at[d], dev(z, mod(x + d, NX), y, c))

    fori(1, NX, lambda d: df(d, x).start())
    w_forward(4)
    fori(1, NX, lambda d: df(d, mod(x - d, NX)).wait_recv())
    dmat[...] = jnp.zeros_like(dmat)
    for r in range(4):
        for h in range(GROUP):
            dmat[r : r + 1, h * HD : (h + 1) * HD] = dfin[r, h : h + 1, :]
    w_forward(5)
    fori(1, NX, lambda d: a_copy(d, mod(x - d, NX)).wait_recv())
    w_forward(6)
    w_forward(7)
    w_forward(8)

    cs_dec[...] = jnp.zeros_like(cs_dec)
    co_dec[...] = jnp.zeros_like(co_dec)

    def product(g, cc, main, dec):
        a = abuf[...].reshape(4 * 128, KW)
        db = dmat[...].astype(BF16)
        for j in range(2):
            wt = wbuf[g * 4 + cc * 2 + j]
            main[j * WC : (j + 1) * WC, :] = lax.dot_general(wt, a, NT, preferred_element_type=F32)
            dd = lax.dot_general(db, wt, NT, preferred_element_type=F32)
            dec[j * 8 : j * 8 + 8, 0:WC] = dd[0:8]

    def cm(d):
        return rcopy(cs_main.at[d], cr_main.at[d], cm_s.at[d], cm_r.at[d], dev(z, x, y, 1 - c))

    def cd(d):
        return rcopy(cs_dec.at[d], cr_dec.at[d], cd_s.at[d], cd_r.at[d], dev(z, x, y, 1 - c))

    def make(d):
        g = mod(y + d, NY)
        product(g, 1 - c, cs_main.at[d], cs_dec.at[d])
        cm(d).start()
        cd(d).start()
        product(g, c, co_main.at[d], co_dec.at[d])

    def r_copy(d, xx):
        return rcopy(
            msg.at[d * 4 + xx],
            rbuf.at[x * 4 + y],
            r_s.at[d * 4 + xx],
            r_r.at[x * 4 + y],
            dev(z, xx, mod(y + d, NY), c),
        )

    def finish(d):
        cm(d).wait_recv()
        cd(d).wait_recv()
        dec = (co_dec[d] + cr_dec[d]).astype(BF16)
        for xx in range(NX):
            ls = slice(xx * 128, (xx + 1) * 128)
            msg[d * 4 + xx, 0:160, :] = (co_main[d, :, ls] + cr_main[d, :, ls]).astype(BF16)
            msg[d * 4 + xx, 160:176, :] = dec

        def go(xx):
            @pl.when((d != 0) | (xx != x))
            def _():
                r_copy(d, xx).start()

        fori(0, NX, go)

    def steps(i):
        @pl.when(i < 4)
        def _():
            make(lax.rem(i + 1, NY))

        @pl.when(i > 0)
        def _():
            finish(lax.rem(i, NY))

    fori(0, 5, steps)
    rbuf[x * 4 + y] = msg[x]

    def r_in(p):
        src = lax.rem(x * 4 + y + p, 16)
        return rcopy(msg.at[0], rbuf.at[src], r_s.at[0], r_r.at[src], dev(z, x, y, 1 - c))

    fori(1, 16, lambda p: r_in(p).wait_recv())

    dlane = lax.broadcasted_iota(jnp.int32, (8, HD), 1)
    dproj = jnp.zeros((8, KW), F32)
    for xs in range(NX):
        tot = rbuf[xs * 4].astype(F32)
        for ys in range(1, NY):
            tot += rbuf[xs * 4 + ys].astype(F32)
        for j in range(2):
            blk = j * 4 + xs
            big[blk * WC : (blk + 1) * WC, :] = tot[j * WC : (j + 1) * WC, :]
            piece = jnp.where(dlane < WC, tot[160 + j * 8 : 168 + j * 8, :], 0.0)
            wide = jnp.concatenate([piece, jnp.zeros((8, KW - HD), F32)], axis=1)
            dproj += pltpu.roll(wide, blk * WC, 1) if blk else wide
    dres = (dhid_ref[...].astype(F32) + dproj[0:4]).astype(BF16)
    dout_ref[...] = dres
    agz[z] = jnp.zeros((8, HD), F32)
    for h in range(GROUP):
        ls = slice(h * HD, (h + 1) * HD)
        res = (hid_ref[:, ls].astype(F32) + big[ls, :].T).astype(BF16)
        out_ref[:, ls] = res
        agz[z, h : h + 1, :] = res.astype(F32)[127:128, :]

    def gz(d, slot):
        return rcopy(agz.at[slot], agz.at[slot], gz_s.at[d], gz_r.at[d], dev(mod(z + d, NZ), x, y, c))

    fori(1, NZ, lambda d: gz(d, z).start())

    def drows(tt):
        return hbuf.at[pl.ds(64, 16), pl.ds(pl.multiple_of(tt * KW, HD), KW)]

    def hrows(xx, tt):
        return hbuf.at[pl.ds(pl.multiple_of(xx * 16, 16), 16), pl.ds(pl.multiple_of(tt * KW, HD), KW)]

    drows(t)[...] = jnp.concatenate([dres.astype(F32), jnp.zeros((12, KW), F32)], axis=0).astype(BF16)

    def dbc(d, yy):
        ref = drows(yy * NC + c)
        return rcopy(ref, ref, db_s.at[d], db_r.at[d], dev(z, x, mod(y + d, NY), c))

    def dcc(d, yy, cc):
        ref = drows(yy * NC + cc)
        return rcopy(ref, ref, dc_s.at[d], dc_r.at[d], dev(z, x, y, 1 - c))

    fori(1, NY, lambda d: dbc(d, y).start())
    dcc(0, y, c).start()

    def dfwd(d):
        yy = mod(y - d, NY)
        dbc(d, yy).wait_recv()
        dcc(d, yy, c).start()

    fori(1, NZ, lambda d: gz(d, mod(z - d, NZ)).wait_recv())
    flat = agz.reshape(NZ * 8, HD)
    for h in range(GROUP):
        rows = flat[pl.ds(h, NZ, stride=8), :].astype(BF16)
        hbuf[pl.ds(pl.multiple_of(x * 16, 16), 16), pl.ds(pl.multiple_of(t * KW + h * HD, HD), HD)] = rows

    def hbc(p, i):
        q = lax.rem(x * 4 + y + p, 16)
        ref = hrows(lax.div(i, 4), lax.rem(i, 4) * NC + c)
        return rcopy(ref, ref, hb_s.at[p], hb_r.at[p], dev(z, lax.div(q, 4), lax.rem(q, 4), c))

    def hcc(p, i, cc):
        ref = hrows(lax.div(i, 4), lax.rem(i, 4) * NC + cc)
        return rcopy(ref, ref, hc_s.at[p], hc_r.at[p], dev(z, x, y, 1 - c))

    fori(1, 16, lambda p: hbc(p, x * 4 + y).start())
    hcc(0, x * 4 + y, c).start()
    fori(1, NY, dfwd)

    def hfwd(p):
        i = lax.rem(x * 4 + y - p + 16, 16)
        hbc(p, i).wait_recv()
        hcc(p, i, c).start()

    fori(1, 16, hfwd)
    fori(0, NY, lambda d: dcc(d, mod(y - d, NY), 1 - c).wait_recv())
    fori(0, 16, lambda p: hcc(p, lax.rem(x * 4 + y - p + 16, 16), 1 - c).wait_recv())
    hw_copy.wait()

    def chunk(i):
        return pl.ds(pl.multiple_of(i * KW, HD), KW)

    def square(i, acc):
        v = hbuf[:, chunk(i)].astype(F32)
        return acc + jnp.sum(v * v, axis=-1, keepdims=True)

    ssq = lax.fori_loop(0, 8, square, jnp.zeros((80, 1), F32))
    inv = lax.rsqrt(ssq / 5120.0 + EPS)
    vocab = hwbuf.shape[1]

    def logit(i, acc):
        v = hbuf[:, chunk(i)].astype(F32)
        n = (v * inv * gain_ref[:, chunk(i)].astype(F32)).astype(BF16)
        return acc + jnp.dot(
            n, hwbuf[pl.ds(pl.multiple_of(i * KW, HD), KW), :], preferred_element_type=F32
        )

    logits = lax.fori_loop(0, 8, logit, jnp.zeros((80, vocab), F32))
    lm = jnp.max(logits, axis=-1, keepdims=True)
    ll = jnp.sum(jnp.exp(logits - lm), axis=-1, keepdims=True)

    ln = lax.broadcasted_iota(jnp.int32, (80, HD), 1)
    tmat[...] = jnp.zeros_like(tmat)
    tmat[0:80, :] = jnp.where(ln == 0, lm, jnp.where(ln == 1, ll, 0.0))
    me = x * 8 + t
    lst[me] = tmat[...].T[0:8, :]

    def lsc(p, i):
        return rcopy(lst.at[i], lst.at[i], ls_s.at[p], ls_r.at[p], plane(p))

    fori(1, 32, lambda p: lsc(p, me).start())
    fori(1, 32, lambda p: lsc(p, lax.rem(me - p + 32, 32)).wait_recv())

    def join(ref, n):
        f = ref.reshape(n * 8, HD)
        ms = f[pl.ds(0, n, stride=8), :]
        lls = f[pl.ds(1, n, stride=8), :]
        top = jnp.max(ms, axis=0, keepdims=True)
        return top, jnp.sum(lls * jnp.exp(ms - top), axis=0, keepdims=True)

    top, tot = join(lst, 32)
    r8 = lax.broadcasted_iota(jnp.int32, (8, HD), 0)
    lsz[z] = jnp.where(r8 == 0, top, tot)

    def lzc(d, i):
        return rcopy(lsz.at[i], lsz.at[i], lz_s.at[d], lz_r.at[d], dev(mod(z + d, NZ), x, y, c))

    fori(1, NZ, lambda d: lzc(d, z).start())
    fori(1, NZ, lambda d: lzc(d, mod(z - d, NZ)).wait_recv())
    top, tot = join(lsz, NZ)
    tmat[...] = jnp.broadcast_to(top + jnp.log(tot), (HD, HD))
    lse = tmat[...].T[0:80, 0:1]
    lp = logits - lse
    lp_ref[0:4, :] = lp[64:68]
    for i in range(64):
        xx, zz = i // 16, i % 16
        lp_ref[4 + zz * 4 + xx : 5 + zz * 4 + xx, :] = lp[i : i + 1]

    for k in range(1, 9):
        w_right(k).wait_send()
    for k in range(1, 8):
        w_left(k).wait_send()

    def three(d):
        dx(d).wait_send()
        a_copy(d, x).wait_send()
        d1(d, zl).wait_send()
        d2(d, zg).wait_send()
        df(d, x).wait_send()
        dbc(d, y).wait_send()

    fori(1, 4, three)

    def four(d):
        cm(d).wait_send()
        cd(d).wait_send()
        dcc(d, mod(y - d, NY), c).wait_send()

        def one(xx):
            @pl.when((d != 0) | (xx != x))
            def _():
                r_copy(d, xx).wait_send()

        fori(0, NX, one)

    fori(0, 4, four)

    def fifteen(d):
        gz(d, z).wait_send()
        hbc(d, x * 4 + y).wait_send()
        lzc(d, z).wait_send()

    fori(1, 16, fifteen)
    fori(0, 16, lambda p: hcc(p, lax.rem(x * 4 + y - p + 16, 16), c).wait_send())
    fori(1, 32, lambda p: lsc(p, me).wait_send())


def local(
    prefill_hidden,
    prefill_query_rows,
    prefill_key_value,
    request_prefix_cache,
    prefix_lengths,
    decode_hidden,
    decode_query_rows,
    decode_kv,
    decode_slot_cache,
    cache_lengths,
    slot_table,
    out_weight,
    final_gain,
    head_weight,
):
    vocab = head_weight.shape[1]
    vm = pl.BlockSpec(memory_space=pltpu.VMEM)
    sm = pl.BlockSpec(memory_space=pltpu.SMEM)
    dma = lambda n: pltpu.SemaphoreType.DMA((n,))
    sems = []
    for n in (9, 8, 4, 4, 4, 4, 4, 4, 4, 16, 16, 16, 16, 4, 4, 32, 16):
        sems += [dma(n), dma(n)]
    return pl.pallas_call(
        kernel,
        out_shape=(
            jax.ShapeDtypeStruct((128, KW), BF16),
            jax.ShapeDtypeStruct((4, KW), BF16),
            jax.ShapeDtypeStruct((68, vocab), F32),
        ),
        in_specs=[sm, sm, sm] + [vm] * 10 + [pl.BlockSpec(memory_space=pl.ANY)],
        out_specs=(vm, vm, vm),
        scratch_shapes=[
            pltpu.VMEM(head_weight.shape, BF16),
            pltpu.VMEM((NZ, WC, KW), BF16),
            pltpu.VMEM((NX, 128, KW), BF16),
            pltpu.VMEM((32, HD), F32),
            pltpu.VMEM((4, 16, HD), F32),
            pltpu.VMEM((4, 16, HD), F32),
            pltpu.VMEM((4, 16, HD), F32),
            pltpu.VMEM((4, 16, HD), F32),
            pltpu.VMEM((4, 8, HD), F32),
            pltpu.VMEM((16, KW), F32),
            pltpu.VMEM((4, 160, 512), F32),
            pltpu.VMEM((4, 16, HD), F32),
            pltpu.VMEM((4, 160, 512), F32),
            pltpu.VMEM((4, 16, HD), F32),
            pltpu.VMEM((4, 160, 512), F32),
            pltpu.VMEM((4, 16, HD), F32),
            pltpu.VMEM((16, 176, HD), BF16),
            pltpu.VMEM((16, 176, HD), BF16),
            pltpu.VMEM((KW, HD), F32),
            pltpu.VMEM((NZ, 8, HD), F32),
            pltpu.VMEM((80, 5120), BF16),
            pltpu.VMEM((HD, HD), F32),
            pltpu.VMEM((32, 8, HD), F32),
            pltpu.VMEM((NZ, 8, HD), F32),
            pltpu.SemaphoreType.DMA,
            *sems,
        ],
        compiler_params=pltpu.CompilerParams(
            collective_id=0, has_side_effects=True, vmem_limit_bytes=48 * 1024 * 1024
        ),
    )(
        prefix_lengths,
        cache_lengths,
        slot_table,
        prefill_hidden,
        prefill_query_rows,
        prefill_key_value,
        request_prefix_cache,
        decode_hidden,
        decode_query_rows,
        decode_kv,
        decode_slot_cache,
        out_weight,
        final_gain.reshape(1, -1),
        head_weight,
    )


def solution(mesh):
    return jax.shard_map(
        local,
        mesh=mesh,
        in_specs=(
            P("seq", "tp"),
            P("seq", "tp"),
            P(None, "seq", "tp"),
            P(None, "seq", None, "tp"),
            P(),
            P(None, "tp"),
            P(None, "tp"),
            P(None, None, "tp"),
            P(None, None, "seq", "tp"),
            P(),
            P(),
            P("tp", "seq"),
            P(),
            P(None, ("seq", "tp")),
        ),
        out_specs=(P("seq", "tp"), P(None, "tp"), P(None, ("seq", "tp"))),
        check_vma=False,
    )
```

time: 1960 us -> 113 us (0.06); the launches traced: 1920 us -> 112 us
  blocking collectives: 724 us -> 0 us
  waiting for transfers between devices: 723 us -> 0 us
  other arithmetic: 385 us -> 0 us
  Pallas kernels: 0 us -> 99.9 us
  local copies, waits for them, and re-layouts: 59 us -> 11.7 us
    unnamed x4 -> x0, waiting for transfers between devices: 449 us -> none
    add x513 -> x0, other arithmetic: 367 us -> none  [the longest x511 366 us: join_totals(): earlier[1] * jnp.exp(earlier[0] - row_max)]
    all_gather x1 -> x0, waiting for transfers between devices: 236 us -> none  [local(): every_row = lax.all_gather(attention_all, 'seq', axis=0, tiled=True)]
    psum x1 -> x0, blocking collectives: 220 us -> none  [local(): lax.psum((decode_sum * factors, decode_mixed * factors[..., None]), 'seq')]
    all_to_all x1 -> x0, blocking collectives: 205 us -> none  [local(): lax.all_to_all(column_block, 'seq', split_axis=0, concat_axis=1, tiled=True)]
    all_gather x2 -> x0, blocking collectives: 177 us -> none  [the longest x1 164 us: local(): lax.all_gather(prefill_out[span_len - 1:], ('seq', 'tp'), axis=0, tiled=T...]
    pmax x1 -> x0, blocking collectives: 123 us -> none  [local(): best = lax.pmax(decode_max, 'seq')]
    pallas_call x0 -> x1, Pallas kernels: none -> 99.9 us  [local(): pl.pallas_call(kernel, out_shape=(jax.ShapeDtypeStruct((128, KW), BF16),...]
  transfers between devices with their start and end apart: 3 -> 0, of which waited for: 3 -> 0; matrix products, arithmetic and copies ran while one was open for 0% -> 0% of each run, Pallas kernels for 0% -> 0%
where the time goes in v1:
time: 113 us; the launch traced here: 112 us
  Pallas kernels  99.9 us (88%)
  local copies, waits for them, and re-layouts  11.7 us (10%)
    pallas_call x1, Pallas kernels, local(): pl.pallas_call(kernel, out_shape=(jax.ShapeDtypeStruct((128, KW), BF16),...  99.9 us
    unnamed x29, local copies, waits for them, and re-layouts  10.9 us

profile of v1, /device:TPU:1, one launch (start us, length us, event | category | flops | bytes accessed | tf_op | source)
XLA Modules:
  0.0 112.4 jit_solution(14107970133356049436)
XLA Ops:
  0.6 0.0 copy-start.11
  0.6 0.0 copy-start.10
  0.7 0.0 copy-start.2
  0.7 0.0 copy-start.8
  0.7 0.0 copy-start.7
  0.7 0.0 copy-start.6
  0.7 0.0 copy-start.9
  0.7 0.0 copy-start.1
  0.7 0.0 copy-start.5
  0.7 0.0 copy-start.4
  0.7 0.0 copy-start.3
  0.7 0.8 reshape.9.gain_ref
  1.6 1.1 copy.17.w_ref
  2.6 5.8 %copy.18.hw_ref = bf16[5120,297]{1,0:T(8,128)(2,1)} copy(bf16[5120,297]{0,1:T(8,128)(2,1)} %param.27) | data formatting | bytes 6082560 | tf_op args[13]
  8.4 0.0 copy-done.11
  8.4 0.0 copy-done.10
  8.4 0.0 copy-done.2
  8.4 0.0 copy-done.8
  8.4 0.0 copy-done.7
  8.4 0.0 copy-done.6
  8.4 0.0 copy-done.9
  8.5 0.0 copy-done.1
  8.5 0.0 copy-done.5
  8.5 0.0 copy-done.4
  8.5 0.0 copy-done.3
  8.5 0.0 copy-start
  8.5 2.1 %copy-done = bf16[5120,297]{1,0:T(8,128)(2,1)S(1)} copy-done((bf16[5120,297]{1,0:T(8,128)(2,1)S(1)}, bf16[5120,297]{1,0:T(8,128)(2,1)}, u32[]{:S(2)}) %copy-start) | copy-done | bytes 3041304
  10.6 99.9 %shard_map.157 = (bf16[128,640]{1,0:T(8,128)(2,1)S(1)}, bf16[4,640]{1,0:T(4,128)(2,1)S(1)}, f32[68,297]{1,0:T(8,128)S(1)}) custom-call(s32[64]{0:T(128)S(1)} %copy-done.9, s32[4]{0:T(128)S(1)} %copy-done.10, s32[4]{0:T(128)S(1)} %copy-done.11, bf16[128,640]{1,0:T(8,128)(2,1)S(1)} %copy-done.3, bf16[128,640]{1,0:T(8,128)(2,1)S(1)} %copy-done.4, ...), custom_call_target="tpu_custom_call" | custom-call | tf_op jit(solution)/shard_map/pallas_call | solution.py:583
  110.5 0.7 copy.22
  111.2 0.6 copy.23
  111.7 0.6 copy.24
Async XLA Ops:
  0.6 7.8 %copy-start.11 = (s32[4]{0:T(128)S(1)}, s32[4]{0:T(128)}, u32[]{:S(2)}) copy-start(s32[4]{0:T(128)} %slot_ref.1) | copy-start | bytes 52
  0.6 7.8 %copy-start.10 = (s32[4]{0:T(128)S(1)}, s32[4]{0:T(128)}, u32[]{:S(2)}) copy-start(s32[4]{0:T(128)} %cache_len_ref.1) | copy-start | bytes 52
  0.7 7.8 %copy-start.2 = (bf16[2,5,128,128]{3,2,1,0:T(8,128)(2,1)S(1)}, bf16[2,5,128,128]{3,2,1,0:T(8,128)(2,1)}, u32[]{:S(2)}) copy-start(bf16[2,5,128,128]{3,2,1,0:T(8,128)(2,1)} %dcache_ref.1) | copy-start | bytes 983044
  0.7 7.8 %copy-start.8 = (bf16[2,4,128]{2,1,0:T(4,128)(2,1)S(1)}, bf16[2,4,128]{2,1,0:T(4,128)(2,1)}, u32[]{:S(2)}) copy-start(bf16[2,4,128]{2,1,0:T(4,128)(2,1)} %dkv_ref.1) | copy-start | bytes 6148
  0.7 7.8 %copy-start.7 = (bf16[4,640]{1,0:T(4,128)(2,1)S(1)}, bf16[4,640]{1,0:T(4,128)(2,1)}, u32[]{:S(2)}) copy-start(bf16[4,640]{1,0:T(4,128)(2,1)} %dq_ref.1) | copy-start | bytes 15364
  0.7 7.8 %copy-start.6 = (bf16[4,640]{1,0:T(4,128)(2,1)S(1)}, bf16[4,640]{1,0:T(4,128)(2,1)}, u32[]{:S(2)}) copy-start(bf16[4,640]{1,0:T(4,128)(2,1)} %dhid_ref.1) | copy-start | bytes 15364
  0.7 7.8 %copy-start.9 = (s32[64]{0:T(128)S(1)}, s32[64]{0:T(128)}, u32[]{:S(2)}) copy-start(s32[64]{0:T(128)} %prefix_len_ref.1) | copy-start | bytes 772
  0.7 7.8 %copy-start.1 = (bf16[2,1,768,128]{3,2,1,0:T(8,128)(2,1)S(1)}, bf16[2,1,768,128]{3,2,1,0:T(8,128)(2,1)}, u32[]{:S(2)}) copy-start(bf16[2,1,768,128]{3,2,1,0:T(8,128)(2,1)} %pre_ref.1) | copy-start | bytes 1179652
  0.7 7.8 %copy-start.5 = (bf16[2,128,128]{2,1,0:T(8,128)(2,1)S(1)}, bf16[2,128,128]{2,1,0:T(8,128)(2,1)}, u32[]{:S(2)}) copy-start(bf16[2,128,128]{2,1,0:T(8,128)(2,1)} %kv_ref.1) | copy-start | bytes 196612
  0.7 7.8 %copy-start.4 = (bf16[128,640]{1,0:T(8,128)(2,1)S(1)}, bf16[128,640]{1,0:T(8,128)(2,1)}, u32[]{:S(2)}) copy-start(bf16[128,640]{1,0:T(8,128)(2,1)} %q_ref.1) | copy-start | bytes 491524
  0.7 7.8 %copy-start.3 = (bf16[128,640]{1,0:T(8,128)(2,1)S(1)}, bf16[128,640]{1,0:T(8,128)(2,1)}, u32[]{:S(2)}) copy-start(bf16[128,640]{1,0:T(8,128)(2,1)} %hid_ref.1) | copy-start | bytes 491524
  8.5 2.1 %copy-start = (bf16[5120,297]{1,0:T(8,128)(2,1)S(1)}, bf16[5120,297]{1,0:T(8,128)(2,1)}, u32[]{:S(2)}) copy-start(bf16[5120,297]{1,0:T(8,128)(2,1)} %copy.18.hw_ref) | copy-start | bytes 9123844

commit v2 on v1

v2 whole, which is shorter than its diff:
```python
import math

import jax
import jax.numpy as jnp
from jax import lax
from jax.experimental import pallas as pl
from jax.experimental.pallas import tpu as pltpu
from jax.sharding import PartitionSpec as P

NEG = -1e30
EPS = 1e-6
NT = (((1,), (1,)), ((), ()))
MESH = pl.DeviceIdType.MESH
F32 = jnp.float32
BF16 = jnp.bfloat16

NX, NY, NZ, NC = 4, 4, 16, 2
NCH = 5
WR = 16
WC = 80
HD = 128
GROUP = 5
KW = 640


def fori(lo, hi, body):
    def step(i, carry):
        body(i)
        return carry

    lax.fori_loop(lo, hi, step, 0)


def mod(a, n):
    return lax.rem(a + n, n)


def kernel(
    prefix_len_ref,
    cache_len_ref,
    slot_ref,
    hid_ref,
    q_ref,
    kv_ref,
    pre_ref,
    dhid_ref,
    dq_ref,
    dkv_ref,
    dcache_ref,
    w_ref,
    gain_ref,
    hw_ref,
    out_ref,
    dout_ref,
    lp_ref,
    hwbuf,
    wbuf,
    abuf,
    qd,
    dpart,
    dxb,
    dz1,
    dz2,
    dfin,
    dmat,
    dtmp,
    lrow,
    rows,
    hres,
    hs_buf,
    hr_buf,
    ho_buf,
    hmsg,
    hrb,
    cs_main,
    cr_main,
    co_main,
    msg,
    rbuf,
    big,
    agz,
    hbuf,
    tmat,
    lst,
    lsz,
    qv,
    prev,
    dcv,
    hw_sem,
    in_sem,
    wr_s,
    wr_r,
    wl_s,
    wl_r,
    a_s,
    a_r,
    dx_s,
    dx_r,
    d1_s,
    d1_r,
    d2_s,
    d2_r,
    df_s,
    df_r,
    lx_s,
    lx_r,
    hx_s,
    hx_r,
    hm_s,
    hm_r,
    cm_s,
    cm_r,
    r_s,
    r_r,
    gz_s,
    gz_r,
    hb_s,
    hb_r,
    hc_s,
    hc_r,
    db_s,
    db_r,
    dc_s,
    dc_r,
    ls_s,
    ls_r,
    lz_s,
    lz_r,
):
    s = lax.axis_index("seq")
    t = lax.axis_index("tp")
    z, x = lax.div(s, NX), lax.rem(s, NX)
    y, c = lax.div(t, NC), lax.rem(t, NC)
    scale = 1.0 / math.sqrt(HD)

    def dev(zz, xx, yy, cc):
        return (zz * NX + xx, yy * NC + cc)

    def rcopy(src, dst, ss, rs, device):
        return pltpu.make_async_remote_copy(
            src_ref=src, dst_ref=dst, send_sem=ss, recv_sem=rs, device_id=device, device_id_type=MESH
        )

    hw_copy = pltpu.make_async_copy(hw_ref, hwbuf, hw_sem)

    barrier = pltpu.get_barrier_semaphore()

    def plane(p):
        q = lax.rem(x * 8 + t + p, 32)
        return (z * NX + lax.div(q, 8), lax.rem(q, 8))

    def sig_z(d):
        pl.semaphore_signal(barrier, inc=1, device_id=dev(mod(z + d, NZ), x, y, c), device_id_type=MESH)

    def sig_p(p):
        pl.semaphore_signal(barrier, inc=1, device_id=plane(p), device_id_type=MESH)

    fori(1, NZ, sig_z)
    fori(1, 32, sig_p)

    w_in = pltpu.make_async_copy(w_ref, wbuf.at[z], in_sem.at[0])
    w_in.start()
    d_in = pltpu.make_async_copy(dcache_ref, dcv, in_sem.at[1])
    d_in.start()
    p_in = pltpu.make_async_copy(pre_ref, prev, in_sem.at[2])
    p_in.start()
    q_in = pltpu.make_async_copy(q_ref, qv, in_sem.at[3])
    q_in.start()
    hw_copy.start()

    w_in.wait()
    pl.semaphore_wait(barrier, NZ - 1 + 31)

    def w_right(k, j):
        b = wbuf.at[mod(z - k + 1, NZ), pl.ds(j * WR, WR)]
        return rcopy(b, b, wr_s.at[k * NCH + j], wr_r.at[k * NCH + j], dev(mod(z + 1, NZ), x, y, c))

    def w_left(k, j):
        b = wbuf.at[mod(z + k - 1, NZ), pl.ds(j * WR, WR)]
        return rcopy(b, b, wl_s.at[k * NCH + j], wl_r.at[k * NCH + j], dev(mod(z - 1, NZ), x, y, c))

    def w_right_in(k, j):
        b = wbuf.at[mod(z - k, NZ), pl.ds(j * WR, WR)]
        return rcopy(b, b, wr_s.at[k * NCH + j], wr_r.at[k * NCH + j], dev(mod(z + 1, NZ), x, y, c))

    def w_left_in(k, j):
        b = wbuf.at[mod(z + k, NZ), pl.ds(j * WR, WR)]
        return rcopy(b, b, wl_s.at[k * NCH + j], wl_r.at[k * NCH + j], dev(mod(z - 1, NZ), x, y, c))

    def w_forward(k):
        def one(j):
            w_right_in(k, j).wait_recv()
            if k < 8:
                w_right(k + 1, j).start()
                w_left_in(k, j).wait_recv()
            if k < 7:
                w_left(k + 1, j).start()

        fori(0, NCH, one)

    def w_first(j):
        w_right(1, j).start()
        w_left(1, j).start()

    fori(0, NCH, w_first)

    qd[...] = jnp.zeros_like(qd)
    dq = dq_ref[...].astype(F32)
    for r in range(4):
        for h in range(GROUP):
            qd[r * 8 + h : r * 8 + h + 1, :] = dq[r : r + 1, h * HD : (h + 1) * HD]
    qall = qd[...].astype(BF16)
    row = lax.broadcasted_iota(jnp.int32, (32, 1), 0)
    rows_slot = jnp.zeros((32, 1), jnp.int32)
    rows_len = jnp.zeros((32, 1), jnp.int32)
    for r in range(4):
        inside = lax.div(row, 8) == r
        rows_slot = jnp.where(inside, slot_ref[r], rows_slot)
        rows_len = jnp.where(inside, cache_len_ref[r], rows_len)
    d_in.wait()
    keys = dcv[0].reshape(5 * 128, HD)
    vals = dcv[1].reshape(5 * 128, HD)
    col = lax.broadcasted_iota(jnp.int32, (32, 640), 1)
    live = (lax.div(col, 128) == rows_slot) & (s * 128 + lax.rem(col, 128) < rows_len)
    sc = lax.dot_general(qall, keys, NT, preferred_element_type=F32) * scale
    sc = jnp.where(live, sc, NEG)
    dm = jnp.max(sc, axis=-1, keepdims=True)
    dw = jnp.where(live, jnp.exp(sc - dm), 0.0)
    dl = jnp.sum(dw, axis=-1, keepdims=True)
    hi = dw.astype(BF16)
    lo = (dw - hi.astype(F32)).astype(BF16)
    do = jnp.dot(hi, vals, preferred_element_type=F32) + jnp.dot(lo, vals, preferred_element_type=F32)
    lane = lax.broadcasted_iota(jnp.int32, (32, HD), 1)
    dstat = jnp.where(lane < 64, dm, dl)
    for r in range(4):
        dpart[r, 0:8, :] = do[r * 8 : r * 8 + 8]
        dpart[r, 8:16, :] = dstat[r * 8 : r * 8 + 8]

    def dx(d):
        xx = mod(x + d, NX)
        return rcopy(dpart.at[xx], dxb.at[x], dx_s.at[d], dx_r.at[d], dev(z, xx, y, c))

    dxb[x] = dpart[x]
    fori(1, NX, lambda d: dx(d).start())

    pe = prefix_len_ref[s]
    p_in.wait()
    q_in.wait()
    kp, ko = prev[0, 0], kv_ref[0]
    vp, vo = prev[1, 0], kv_ref[1]
    n_pre = kp.shape[0]
    live1 = lax.broadcasted_iota(jnp.int32, (128, n_pre), 1) < pe
    live2 = lax.broadcasted_iota(jnp.int32, (128, 128), 1) <= lax.broadcasted_iota(jnp.int32, (128, 128), 0)
    lrow[...] = jnp.zeros_like(lrow)

    def head(h):
        hs = pl.ds(pl.multiple_of(h * HD, HD), HD)
        qh = qv[:, hs]
        s1 = lax.dot_general(qh, kp, NT, preferred_element_type=F32) * scale
        s2 = lax.dot_general(qh, ko, NT, preferred_element_type=F32) * scale
        s1 = jnp.where(live1, s1, NEG)
        s2 = jnp.where(live2, s2, NEG)
        m = jnp.maximum(jnp.max(s1, -1, keepdims=True), jnp.max(s2, -1, keepdims=True))
        p1 = jnp.where(live1, jnp.exp(s1 - m), 0.0)
        p2 = jnp.where(live2, jnp.exp(s2 - m), 0.0)
        total = jnp.sum(p1, -1, keepdims=True) + jnp.sum(p2, -1, keepdims=True)
        o = jnp.dot(p1.astype(BF16), vp, preferred_element_type=F32)
        o += jnp.dot(p2.astype(BF16), vo, preferred_element_type=F32)
        o = (o / total).astype(BF16)
        abuf[x, :, hs] = o
        lrow[pl.ds(h, 1), :] = o.astype(F32)[127:128, :]
        lrow[pl.ds(8 + h, 1), :] = hid_ref[:, hs].astype(F32)[127:128, :]

    fori(0, 2, head)
    w_forward(1)

    def merge(ref):
        os = [ref[i, 0:8, :] for i in range(4)]
        st = [ref[i, 8:16, :] for i in range(4)]
        ms = [a[:, 0:1] for a in st]
        lls = [a[:, 64:65] for a in st]
        m = jnp.maximum(jnp.maximum(ms[0], ms[1]), jnp.maximum(ms[2], ms[3]))
        o, l = 0.0, 0.0
        for i in range(4):
            f = jnp.exp(ms[i] - m)
            o = o + os[i] * f
            l = l + lls[i] * f
        return o, m, l

    lane8 = lax.broadcasted_iota(jnp.int32, (8, HD), 1)

    def dx_in(d):
        return rcopy(dpart.at[x], dxb.at[mod(x - d, NX)], dx_s.at[d], dx_r.at[d], dev(z, mod(x + d, NX), y, c))

    fori(1, NX, lambda d: dx_in(d).wait_recv())
    o, m, l = merge(dxb)
    zl, zg = lax.rem(z, 4), lax.div(z, 4)
    dz1[zl, 0:8, :] = o
    dz1[zl, 8:16, :] = jnp.where(lane8 < 64, m, l)

    def d1(d, slot):
        return rcopy(dz1.at[slot], dz1.at[slot], d1_s.at[d], d1_r.at[d], dev(zg * 4 + mod(zl + d, 4), x, y, c))

    fori(1, 4, lambda d: d1(d, zl).start())
    fori(2, GROUP, head)

    def a_copy(d, src):
        return rcopy(abuf.at[src], abuf.at[src], a_s.at[d], a_r.at[d], dev(z, mod(x + d, NX), y, c))

    def gz(d, slot):
        return rcopy(agz.at[slot], agz.at[slot], gz_s.at[d], gz_r.at[d], dev(mod(z + d, NZ), x, y, c))

    agz[z] = lrow[...].astype(BF16)
    fori(1, NZ, lambda d: gz(d, z).start())
    w_forward(2)
    fori(1, NX, lambda d: a_copy(d, x).start())
    fori(1, 4, lambda d: d1(d, mod(zl - d, 4)).wait_recv())
    o, m, l = merge(dz1)
    dz2[zg, 0:8, :] = o
    dz2[zg, 8:16, :] = jnp.where(lane8 < 64, m, l)

    def d2(d, slot):
        return rcopy(dz2.at[slot], dz2.at[slot], d2_s.at[d], d2_r.at[d], dev(mod(zg + d, 4) * 4 + zl, x, y, c))

    fori(1, 4, lambda d: d2(d, zg).start())
    w_forward(3)
    w_forward(4)
    w_forward(5)

    fori(1, NZ, lambda d: gz(d, mod(z - d, NZ)).wait_recv())
    for i in range(NZ):
        rows[i * 16 : i * 16 + 16, :] = agz[i].astype(F32)
    mine16 = pl.ds(pl.multiple_of(x * 32, 16), 16)
    for h in range(GROUP):
        hs = slice(h * HD, (h + 1) * HD)
        dmat[mine16, hs] = rows[pl.ds(h, NZ, stride=16), :].astype(BF16)
        hres[0:16, hs] = rows[pl.ds(8 + h, NZ, stride=16), :]

    def lx(d, xx):
        ref = dmat.at[pl.ds(pl.multiple_of(xx * 32, 16), 16)]
        return rcopy(ref, ref, lx_s.at[d], lx_r.at[d], dev(z, mod(x + d, NX), y, c))

    fori(1, NX, lambda d: lx(d, x).start())
    w_forward(6)
    fori(1, 4, lambda d: d2(d, mod(zg - d, 4)).wait_recv())
    o, m, l = merge(dz2)
    row4 = lax.broadcasted_iota(jnp.int32, (4, HD), 0)
    own_k = jnp.sum(jnp.where(row4 == x, dkv_ref[0].astype(F32), 0.0), axis=0, keepdims=True)
    own_v = jnp.sum(jnp.where(row4 == x, dkv_ref[1].astype(F32), 0.0), axis=0, keepdims=True)
    own_q = qd[pl.ds(pl.multiple_of(x * 8, 8), 8), :]
    own_s = jnp.sum(own_q * own_k, axis=-1, keepdims=True) * scale
    m2 = jnp.maximum(m, own_s)
    f1, f2 = jnp.exp(m - m2), jnp.exp(own_s - m2)
    dfin[x] = (o * f1 + own_v * f2) / (l * f1 + f2)

    def df(d, slot):
        return rcopy(dfin.at[slot], dfin.at[slot], df_s.at[d], df_r.at[d], dev(z, mod(x + d, NX), y, c))

    fori(1, NX, lambda d: df(d, x).start())
    w_forward(7)
    fori(1, NX, lambda d: a_copy(d, mod(x - d, NX)).wait_recv())
    fori(1, NX, lambda d: lx(d, mod(x - d, NX)).wait_recv())
    fori(1, NX, lambda d: df(d, mod(x - d, NX)).wait_recv())
    dtmp[...] = jnp.zeros_like(dtmp)
    for r in range(4):
        for h in range(GROUP):
            dtmp[r : r + 1, h * HD : (h + 1) * HD] = dfin[r, h : h + 1, :]
    for xx in range(NX):
        dmat[xx * 32 + 16 : xx * 32 + 32, :] = dtmp[...].astype(BF16)
    hs_buf[...] = jnp.zeros_like(hs_buf)
    ho_buf[...] = jnp.zeros_like(ho_buf)
    w_forward(8)

    def head_product(g, cc, dst):
        for j in range(2):
            p = lax.dot_general(dmat[...], wbuf[g * 4 + cc * 2 + j], NT, preferred_element_type=F32)
            for xx in range(NX):
                dst[xx, j * 32 : j * 32 + 32, 0:WC] = p[xx * 32 : xx * 32 + 32]

    def hx(d):
        return rcopy(hs_buf.at[d], hr_buf.at[d], hx_s.at[d], hx_r.at[d], dev(z, x, y, 1 - c))

    def head_other(d):
        head_product(mod(y + d, NY), 1 - c, hs_buf.at[d])
        hx(d).start()

    fori(0, NY, head_other)
    fori(0, NY, lambda d: head_product(mod(y + d, NY), c, ho_buf.at[d]))

    def hm(d, xx):
        return rcopy(
            hmsg.at[d, xx],
            hrb.at[x * 4 + y],
            hm_s.at[d * 4 + xx],
            hm_r.at[x * 4 + y],
            dev(z, xx, mod(y + d, NY), c),
        )

    def away(fn):
        def each(d, xx):
            @pl.when((d != 0) | (xx != x))
            def _():
                fn(d, xx)

        return lambda i: each(lax.div(i, 4), lax.rem(i, 4))

    def head_send(i):
        d = lax.rem(i + 1, NY)
        hx(d).wait_recv()
        hmsg[d] = (ho_buf[d] + hr_buf[d]).astype(BF16)
        fori(d * 4, d * 4 + 4, away(lambda d, xx: hm(d, xx).start()))

    fori(0, NY, head_send)
    hrb[x * 4 + y] = hmsg[0, x]

    def product(g, cc, main):
        a = abuf[...].reshape(4 * 128, KW)
        wt = wbuf[pl.ds(g * 4 + cc * 2, 2)].reshape(2 * WC, KW)
        main[...] = lax.dot_general(wt, a, NT, preferred_element_type=F32)

    def cm(d):
        return rcopy(cs_main.at[d], cr_main.at[d], cm_s.at[d], cm_r.at[d], dev(z, x, y, 1 - c))

    def make(d):
        product(mod(y + d, NY), 1 - c, cs_main.at[d])
        cm(d).start()

    fori(0, NY, make)

    def hm_in(p):
        src = lax.rem(x * 4 + y + p, 16)
        return rcopy(hmsg.at[0, 0], hrb.at[src], hm_s.at[0], hm_r.at[src], dev(z, x, y, 1 - c))

    fori(1, 16, lambda p: hm_in(p).wait_recv())
    hlane = lax.broadcasted_iota(jnp.int32, (32, HD), 1)
    hproj = jnp.zeros((32, KW), F32)
    for xs in range(NX):
        tot = hrb[xs * 4].astype(F32)
        for ys in range(1, NY):
            tot += hrb[xs * 4 + ys].astype(F32)
        for j in range(2):
            blk = j * 4 + xs
            piece = jnp.where(hlane < WC, tot[j * 32 : j * 32 + 32, :], 0.0)
            wide = jnp.concatenate([piece, jnp.zeros((32, KW - HD), F32)], axis=1)
            hproj += pltpu.roll(wide, blk * WC, 1) if blk else wide

    def drows(tt):
        return hbuf.at[pl.ds(64, 16), pl.ds(pl.multiple_of(tt * KW, HD), KW)]

    def hrows(xx, tt):
        return hbuf.at[pl.ds(pl.multiple_of(xx * 16, 16), 16), pl.ds(pl.multiple_of(tt * KW, HD), KW)]

    hrows(x, t)[...] = (hres[0:16, :] + hproj[0:16]).astype(BF16)

    def hbc(p, i):
        q = lax.rem(x * 4 + y + p, 16)
        ref = hrows(lax.div(i, 4), lax.rem(i, 4) * NC + c)
        return rcopy(ref, ref, hb_s.at[p], hb_r.at[p], dev(z, lax.div(q, 4), lax.rem(q, 4), c))

    def hcc(p, i, cc):
        ref = hrows(lax.div(i, 4), lax.rem(i, 4) * NC + cc)
        return rcopy(ref, ref, hc_s.at[p], hc_r.at[p], dev(z, x, y, 1 - c))

    def dbc(d, yy):
        ref = drows(yy * NC + c)
        return rcopy(ref, ref, db_s.at[d], db_r.at[d], dev(z, x, mod(y + d, NY), c))

    def dcc(d, yy, cc):
        ref = drows(yy * NC + cc)
        return rcopy(ref, ref, dc_s.at[d], dc_r.at[d], dev(z, x, y, 1 - c))

    fori(1, 16, lambda p: hbc(p, x * 4 + y).start())
    hcc(0, x * 4 + y, c).start()
    dres = (dhid_ref[...].astype(F32) + hproj[16:20]).astype(BF16)
    dout_ref[...] = dres
    drows(t)[...] = jnp.concatenate([dres.astype(F32), jnp.zeros((12, KW), F32)], axis=0).astype(BF16)
    fori(1, NY, lambda d: dbc(d, y).start())
    dcc(0, y, c).start()

    fori(0, NY, lambda d: product(mod(y + d, NY), c, co_main.at[d]))

    def finish(d):
        cm(d).wait_recv()
        for xx in range(NX):
            ls = slice(xx * 128, (xx + 1) * 128)
            msg[d * 4 + xx] = (co_main[d, :, ls] + cr_main[d, :, ls]).astype(BF16)

    fori(0, NY, finish)

    def hfwd(p):
        i = lax.rem(x * 4 + y - p + 16, 16)
        hbc(p, i).wait_recv()
        hcc(p, i, c).start()

    fori(1, 16, hfwd)

    def dfwd(d):
        yy = mod(y - d, NY)
        dbc(d, yy).wait_recv()
        dcc(d, yy, c).start()

    fori(1, NY, dfwd)

    def r_copy(d, xx):
        return rcopy(
            msg.at[d * 4 + xx],
            rbuf.at[x * 4 + y],
            r_s.at[d * 4 + xx],
            r_r.at[x * 4 + y],
            dev(z, xx, mod(y + d, NY), c),
        )

    fori(4, 20, lambda i: away(lambda d, xx: r_copy(d, xx).start())(lax.rem(i, 16)))
    rbuf[x * 4 + y] = msg[x]
    fori(0, NY, lambda d: dcc(d, mod(y - d, NY), 1 - c).wait_recv())
    fori(0, 16, lambda p: hcc(p, lax.rem(x * 4 + y - p + 16, 16), 1 - c).wait_recv())
    hw_copy.wait()

    def chunk(i):
        return pl.ds(pl.multiple_of(i * KW, HD), KW)

    def square(i, acc):
        v = hbuf[:, chunk(i)].astype(F32)
        return acc + jnp.sum(v * v, axis=-1, keepdims=True)

    ssq = lax.fori_loop(0, 8, square, jnp.zeros((80, 1), F32))
    inv = lax.rsqrt(ssq / 5120.0 + EPS)
    vocab = hwbuf.shape[0]

    def logit(i, acc):
        v = hbuf[:, chunk(i)].astype(F32)
        n = (v * inv * gain_ref[:, chunk(i)].astype(F32)).astype(BF16)
        return acc + lax.dot_general(n, hwbuf[:, chunk(i)], NT, preferred_element_type=F32)

    logits = lax.fori_loop(0, 8, logit, jnp.zeros((80, vocab), F32))
    lm = jnp.max(logits, axis=-1, keepdims=True)
    ll = jnp.sum(jnp.exp(logits - lm), axis=-1, keepdims=True)

    ln = lax.broadcasted_iota(jnp.int32, (80, HD), 1)
    tmat[...] = jnp.zeros_like(tmat)
    tmat[0:80, :] = jnp.where(ln == 0, lm, jnp.where(ln == 1, ll, 0.0))
    me = x * 8 + t
    lsz[z] = tmat[...].T[0:8, :]

    def lzc(d, i):
        return rcopy(lsz.at[i], lsz.at[i], lz_s.at[d], lz_r.at[d], dev(mod(z + d, NZ), x, y, c))

    def lsc(p, i):
        return rcopy(lst.at[i], lst.at[i], ls_s.at[p], ls_r.at[p], plane(p))

    def join(ref, n):
        f = ref.reshape(n * 8, HD)
        ms = f[pl.ds(0, n, stride=8), :]
        lls = f[pl.ds(1, n, stride=8), :]
        top = jnp.max(ms, axis=0, keepdims=True)
        return top, jnp.sum(lls * jnp.exp(ms - top), axis=0, keepdims=True)

    fori(1, NZ, lambda d: lzc(d, z).start())

    def r_in(p):
        src = lax.rem(x * 4 + y + p, 16)
        return rcopy(msg.at[0], rbuf.at[src], r_s.at[0], r_r.at[src], dev(z, x, y, 1 - c))

    fori(1, 16, lambda p: r_in(p).wait_recv())
    for xs in range(NX):
        tot = rbuf[xs * 4].astype(F32)
        for ys in range(1, NY):
            tot += rbuf[xs * 4 + ys].astype(F32)
        for j in range(2):
            blk = j * 4 + xs
            big[blk * WC : (blk + 1) * WC, :] = tot[j * WC : (j + 1) * WC, :]
    for h in range(GROUP):
        ls = slice(h * HD, (h + 1) * HD)
        out_ref[:, ls] = (hid_ref[:, ls].astype(F32) + big[ls, :].T).astype(BF16)

    fori(1, NZ, lambda d: lzc(d, mod(z - d, NZ)).wait_recv())
    top, tot = join(lsz, NZ)
    r8 = lax.broadcasted_iota(jnp.int32, (8, HD), 0)
    lst[me] = jnp.where(r8 == 0, top, tot)
    fori(1, 32, lambda p: lsc(p, me).start())
    fori(1, 32, lambda p: lsc(p, lax.rem(me - p + 32, 32)).wait_recv())
    top, tot = join(lst, 32)
    tmat[...] = jnp.broadcast_to(top + jnp.log(tot), (HD, HD))
    lse = tmat[...].T[0:80, 0:1]
    lp = logits - lse
    lp_ref[0:4, :] = lp[64:68]
    for i in range(64):
        xx, zz = i // 16, i % 16
        lp_ref[4 + zz * 4 + xx : 5 + zz * 4 + xx, :] = lp[i : i + 1]

    def ring(i):
        w_right(lax.div(i, NCH), lax.rem(i, NCH)).wait_send()

        @pl.when(i < 8 * NCH)
        def _():
            w_left(lax.div(i, NCH), lax.rem(i, NCH)).wait_send()

    fori(NCH, 9 * NCH, ring)

    def three(d):
        dx(d).wait_send()
        a_copy(d, x).wait_send()
        lx(d, x).wait_send()
        d1(d, zl).wait_send()
        d2(d, zg).wait_send()
        df(d, x).wait_send()
        dbc(d, y).wait_send()

    fori(1, 4, three)

    def four(d):
        hx(d).wait_send()
        cm(d).wait_send()
        dcc(d, mod(y - d, NY), c).wait_send()

    fori(0, 4, four)

    def leave(d, xx):
        hm(d, xx).wait_send()
        r_copy(d, xx).wait_send()

    fori(0, 16, away(leave))

    def fifteen(d):
        gz(d, z).wait_send()
        hbc(d, x * 4 + y).wait_send()
        lzc(d, z).wait_send()

    fori(1, 16, fifteen)
    fori(0, 16, lambda p: hcc(p, lax.rem(x * 4 + y - p + 16, 16), c).wait_send())
    fori(1, 32, lambda p: lsc(p, me).wait_send())


def local(
    prefill_hidden,
    prefill_query_rows,
    prefill_key_value,
    request_prefix_cache,
    prefix_lengths,
    decode_hidden,
    decode_query_rows,
    decode_kv,
    decode_slot_cache,
    cache_lengths,
    slot_table,
    out_weight,
    final_gain,
    head_weight,
):
    vocab = head_weight.shape[1]
    vm = pl.BlockSpec(memory_space=pltpu.VMEM)
    sm = pl.BlockSpec(memory_space=pltpu.SMEM)
    hbm = pl.BlockSpec(memory_space=pl.ANY)
    dma = lambda n: pltpu.SemaphoreType.DMA((n,))
    sems = []
    for n in (9 * NCH, 8 * NCH, 4, 4, 4, 4, 4, 4, 4, 16, 4, 16, 16, 16, 16, 4, 4, 32, 16):
        sems += [dma(n), dma(n)]
    return pl.pallas_call(
        kernel,
        out_shape=(
            jax.ShapeDtypeStruct((128, KW), BF16),
            jax.ShapeDtypeStruct((4, KW), BF16),
            jax.ShapeDtypeStruct((68, vocab), F32),
        ),
        in_specs=[sm, sm, sm, vm, hbm, vm, hbm, vm, vm, vm, hbm, hbm, vm, hbm],
        out_specs=(vm, vm, vm),
        scratch_shapes=[
            pltpu.VMEM(head_weight.shape[::-1], BF16),
            pltpu.VMEM((NZ, WC, KW), BF16),
            pltpu.VMEM((NX, 128, KW), BF16),
            pltpu.VMEM((32, HD), F32),
            pltpu.VMEM((4, 16, HD), F32),
            pltpu.VMEM((4, 16, HD), F32),
            pltpu.VMEM((4, 16, HD), F32),
            pltpu.VMEM((4, 16, HD), F32),
            pltpu.VMEM((4, 8, HD), F32),
            pltpu.VMEM((128, KW), BF16),
            pltpu.VMEM((16, KW), F32),
            pltpu.VMEM((16, HD), F32),
            pltpu.VMEM((NZ * 16, HD), F32),
            pltpu.VMEM((16, KW), F32),
            pltpu.VMEM((NY, NX, 64, HD), F32),
            pltpu.VMEM((NY, NX, 64, HD), F32),
            pltpu.VMEM((NY, NX, 64, HD), F32),
            pltpu.VMEM((NY, NX, 64, HD), BF16),
            pltpu.VMEM((16, 64, HD), BF16),
            pltpu.VMEM((4, 160, 512), F32),
            pltpu.VMEM((4, 160, 512), F32),
            pltpu.VMEM((4, 160, 512), F32),
            pltpu.VMEM((16, 160, HD), BF16),
            pltpu.VMEM((16, 160, HD), BF16),
            pltpu.VMEM((KW, HD), F32),
            pltpu.VMEM((NZ, 16, HD), BF16),
            pltpu.VMEM((80, 5120), BF16),
            pltpu.VMEM((HD, HD), F32),
            pltpu.VMEM((32, 8, HD), F32),
            pltpu.VMEM((NZ, 8, HD), F32),
            pltpu.VMEM((128, KW), BF16),
            pltpu.VMEM((2, 1, 768, HD), BF16),
            pltpu.VMEM((2, 5, 128, HD), BF16),
            pltpu.SemaphoreType.DMA,
            dma(4),
            *sems,
        ],
        compiler_params=pltpu.CompilerParams(
            collective_id=0, has_side_effects=True, vmem_limit_bytes=60 * 1024 * 1024
        ),
    )(
        prefix_lengths,
        cache_lengths,
        slot_table,
        prefill_hidden,
        prefill_query_rows,
        prefill_key_value,
        request_prefix_cache,
        decode_hidden,
        decode_query_rows,
        decode_kv,
        decode_slot_cache,
        out_weight.T,
        final_gain.reshape(1, -1),
        head_weight.T,
    )


def solution(mesh):
    return jax.shard_map(
        local,
        mesh=mesh,
        in_specs=(
            P("seq", "tp"),
            P("seq", "tp"),
            P(None, "seq", "tp"),
            P(None, "seq", None, "tp"),
            P(),
            P(None, "tp"),
            P(None, "tp"),
            P(None, None, "tp"),
            P(None, None, "seq", "tp"),
            P(),
            P(),
            P("tp", "seq"),
            P(),
            P(None, ("seq", "tp")),
        ),
        out_specs=(P("seq", "tp"), P(None, "tp"), P(None, ("seq", "tp"))),
        check_vma=False,
    )
```

time: 113 us -> 92.5 us (0.82)
  Pallas kernels: 99.9 us -> 85.8 us
  local copies, waits for them, and re-layouts: 11.7 us -> 5.75 us
    pallas_call x1, Pallas kernels: 99.9 us -> 85.8 us  [local(): pl.pallas_call(kernel, out_shape=(jax.ShapeDtypeStruct((128, KW), BF16),...]
    unnamed x29 -> x3, local copies, waits for them, and re-layouts: 10.9 us -> 4.43 us
where the time goes in v2:
time: 92.5 us; the launch traced here: 92.2 us
  Pallas kernels  85.8 us (93%)
  local copies, waits for them, and re-layouts  5.75 us (6%)
    pallas_call x1, Pallas kernels, local(): pl.pallas_call(kernel, out_shape=(jax.ShapeDtypeStruct((128, KW), BF16),...  85.8 us
    unnamed x3, local copies, waits for them, and re-layouts  4.43 us

profile of v2, /device:TPU:1, one launch (start us, length us, event | category | flops | bytes accessed | tf_op | source)
XLA Modules:
  0.0 92.2 jit_solution(16198750212614554363)
XLA Ops:
  0.6 1.3 %reshape.9.gain_ref = bf16[1,5120]{1,0:T(2,128)(2,1)} reshape(bf16[5120]{0:T(1024)(128)(2,1)} %param.26) | data formatting | bytes 20480 | tf_op jit(solution)/shard_map/reshape | solution.py:721
  2.0 85.8 %shard_map.157 = (bf16[128,640]{1,0:T(8,128)(2,1)}, bf16[4,640]{1,0:T(4,128)(2,1)}, f32[68,297]{1,0:T(8,128)}) custom-call(s32[64]{0:T(128)} %prefix_len_ref.1, s32[4]{0:T(128)} %cache_len_ref.1, s32[4]{0:T(128)} %slot_ref.1, bf16[128,640]{1,0:T(8,128)(2,1)} %hid_ref.1, bf16[128,640]{1,0:T(8,128)(2,1)} %q_ref.1, bf16[2,128,128]{2,1,0:T(8,128)(2,1)} %kv_ref.1, ...), custom_call_target="tpu_custom_call" | custom-call | tf_op jit(solution)/shard_map/pallas_call | solution.py:658
  87.8 1.6 %copy.20 = bf16[128,640]{1,0:T(8,128)(2,1)} copy(bf16[128,640]{1,0:T(8,128)(2,1)} %get-tuple-element.6) | data formatting | bytes 327680
  89.4 1.3 %copy.21 = bf16[4,640]{1,0:T(4,128)(2,1)} copy(bf16[4,640]{1,0:T(4,128)(2,1)} %get-tuple-element.7) | data formatting | bytes 10240
  90.7 1.5 %copy.22 = f32[68,297]{1,0:T(8,128)} copy(f32[68,297]{1,0:T(8,128)} %get-tuple-element.8) | data formatting | bytes 161568

commit v3 on v2

--- a/solution.py
+++ b/solution.py
@@ -36,20 +36,20 @@
 
 
 def kernel(
-    prefix_len_ref,
-    cache_len_ref,
-    slot_ref,
-    hid_ref,
-    q_ref,
-    kv_ref,
-    pre_ref,
-    dhid_ref,
-    dq_ref,
-    dkv_ref,
-    dcache_ref,
-    w_ref,
-    gain_ref,
-    hw_ref,
+    prefix_len_hbm,
+    cache_len_hbm,
+    slot_hbm,
+    hid_hbm,
+    q_hbm,
+    kv_hbm,
+    pre_hbm,
+    dhid_hbm,
+    dq_hbm,
+    dkv_hbm,
+    dcache_hbm,
+    w_hbm,
+    gain_hbm,
+    hw_hbm,
     out_ref,
     dout_ref,
     lp_ref,
@@ -67,14 +67,12 @@
     lrow,
     rows,
     hres,
-    hs_buf,
+    h_buf,
     hr_buf,
-    ho_buf,
     hmsg,
     hrb,
     cs_main,
     cr_main,
-    co_main,
     msg,
     rbuf,
     big,
@@ -83,10 +81,20 @@
     tmat,
     lst,
     lsz,
+    lpad,
     qv,
     prev,
     dcv,
-    hw_sem,
+    prefix_len_ref,
+    cache_len_ref,
+    slot_ref,
+    hid_ref,
+    kv_ref,
+    dhid_ref,
+    dq_ref,
+    dkv_ref,
+    gain_ref,
+    gain2,
     in_sem,
     wr_s,
     wr_r,
@@ -141,8 +149,6 @@
             src_ref=src, dst_ref=dst, send_sem=ss, recv_sem=rs, device_id=device, device_id_type=MESH
         )
 
-    hw_copy = pltpu.make_async_copy(hw_ref, hwbuf, hw_sem)
-
     barrier = pltpu.get_barrier_semaphore()
 
     def plane(p):
@@ -158,16 +164,25 @@
     fori(1, NZ, sig_z)
     fori(1, 32, sig_p)
 
-    w_in = pltpu.make_async_copy(w_ref, wbuf.at[z], in_sem.at[0])
-    w_in.start()
-    d_in = pltpu.make_async_copy(dcache_ref, dcv, in_sem.at[1])
-    d_in.start()
-    p_in = pltpu.make_async_copy(pre_ref, prev, in_sem.at[2])
-    p_in.start()
-    q_in = pltpu.make_async_copy(q_ref, qv, in_sem.at[3])
-    q_in.start()
-    hw_copy.start()
-
+    def bring(i, src, dst):
+        copy = pltpu.make_async_copy(src, dst, in_sem.at[i])
+        copy.start()
+        return copy
+
+    w_in = bring(0, w_hbm, wbuf.at[z])
+    dq_in = bring(1, dq_hbm, dq_ref)
+    slot_in = bring(2, slot_hbm, slot_ref)
+    clen_in = bring(3, cache_len_hbm, cache_len_ref)
+    d_in = bring(4, dcache_hbm, dcv)
+    plen_in = bring(5, prefix_len_hbm, prefix_len_ref)
+    p_in = bring(6, pre_hbm, prev)
+    q_in = bring(7, q_hbm, qv)
+    kv_in = bring(8, kv_hbm, kv_ref)
+    hid_in = bring(9, hid_hbm, hid_ref)
+    dkv_in = bring(10, dkv_hbm, dkv_ref)
+    dhid_in = bring(11, dhid_hbm, dhid_ref)
+    gain_in = bring(12, gain_hbm, gain_ref)
+    hw_copy = bring(13, hw_hbm, hwbuf)
     w_in.wait()
     pl.semaphore_wait(barrier, NZ - 1 + 31)
 
@@ -190,13 +205,32 @@
     def w_forward(k):
         def one(j):
             w_right_in(k, j).wait_recv()
-            if k < 8:
-                w_right(k + 1, j).start()
-                w_left_in(k, j).wait_recv()
-            if k < 7:
-                w_left(k + 1, j).start()
-
-        fori(0, NCH, one)
+            w_right(k + 1, j).start()
+            w_left_in(k, j).wait_recv()
+            w_left(k + 1, j).start()
+
+        def turn(j):
+            w_right_in(7, j).wait_recv()
+            w_left_in(7, j).wait_recv()
+
+            @pl.when(j < 3)
+            def _():
+                w_right(8, j).start()
+
+            @pl.when(j >= 3)
+            def _():
+                w_left(8, j).start()
+
+        def last(j):
+            @pl.when(j < 3)
+            def _():
+                w_right_in(8, j).wait_recv()
+
+            @pl.when(j >= 3)
+            def _():
+                w_left_in(8, j).wait_recv()
+
+        fori(0, NCH, one if k < 7 else turn if k == 7 else last)
 
     def w_first(j):
         w_right(1, j).start()
@@ -205,6 +239,9 @@
     fori(0, NCH, w_first)
 
     qd[...] = jnp.zeros_like(qd)
+    dq_in.wait()
+    slot_in.wait()
+    clen_in.wait()
     dq = dq_ref[...].astype(F32)
     for r in range(4):
         for h in range(GROUP):
@@ -243,9 +280,12 @@
     dxb[x] = dpart[x]
     fori(1, NX, lambda d: dx(d).start())
 
-    pe = prefix_len_ref[s]
+    plen_in.wait()
     p_in.wait()
     q_in.wait()
+    kv_in.wait()
+    hid_in.wait()
+    pe = prefix_len_ref[s]
     kp, ko = prev[0, 0], kv_ref[0]
     vp, vo = prev[1, 0], kv_ref[1]
     n_pre = kp.shape[0]
@@ -271,8 +311,6 @@
         lrow[pl.ds(h, 1), :] = o.astype(F32)[127:128, :]
         lrow[pl.ds(8 + h, 1), :] = hid_ref[:, hs].astype(F32)[127:128, :]
 
-    fori(0, 2, head)
-    w_forward(1)
 
     def merge(ref):
         os = [ref[i, 0:8, :] for i in range(4)]
@@ -292,9 +330,17 @@
     def dx_in(d):
         return rcopy(dpart.at[x], dxb.at[mod(x - d, NX)], dx_s.at[d], dx_r.at[d], dev(z, mod(x + d, NX), y, c))
 
+    zl, zg = lax.rem(z, 4), lax.div(z, 4)
+    def heads(h):
+        head(h)
+
+        @pl.when(h == 2)
+        def _():
+            w_forward(1)
+
+    fori(0, GROUP, heads)
     fori(1, NX, lambda d: dx_in(d).wait_recv())
     o, m, l = merge(dxb)
-    zl, zg = lax.rem(z, 4), lax.div(z, 4)
     dz1[zl, 0:8, :] = o
     dz1[zl, 8:16, :] = jnp.where(lane8 < 64, m, l)
 
@@ -302,7 +348,6 @@
         return rcopy(dz1.at[slot], dz1.at[slot], d1_s.at[d], d1_r.at[d], dev(zg * 4 + mod(zl + d, 4), x, y, c))
 
     fori(1, 4, lambda d: d1(d, zl).start())
-    fori(2, GROUP, head)
 
     def a_copy(d, src):
         return rcopy(abuf.at[src], abuf.at[src], a_s.at[d], a_r.at[d], dev(z, mod(x + d, NX), y, c))
@@ -344,6 +389,7 @@
     w_forward(6)
     fori(1, 4, lambda d: d2(d, mod(zg - d, 4)).wait_recv())
     o, m, l = merge(dz2)
+    dkv_in.wait()
     row4 = lax.broadcasted_iota(jnp.int32, (4, HD), 0)
     own_k = jnp.sum(jnp.where(row4 == x, dkv_ref[0].astype(F32), 0.0), axis=0, keepdims=True)
     own_v = jnp.sum(jnp.where(row4 == x, dkv_ref[1].astype(F32), 0.0), axis=0, keepdims=True)
@@ -367,34 +413,53 @@
             dtmp[r : r + 1, h * HD : (h + 1) * HD] = dfin[r, h : h + 1, :]
     for xx in range(NX):
         dmat[xx * 32 + 16 : xx * 32 + 32, :] = dtmp[...].astype(BF16)
-    hs_buf[...] = jnp.zeros_like(hs_buf)
-    ho_buf[...] = jnp.zeros_like(ho_buf)
-    w_forward(8)
-
-    def head_product(g, cc, dst):
-        for j in range(2):
-            p = lax.dot_general(dmat[...], wbuf[g * 4 + cc * 2 + j], NT, preferred_element_type=F32)
-            for xx in range(NX):
-                dst[xx, j * 32 : j * 32 + 32, 0:WC] = p[xx * 32 : xx * 32 + 32]
-
-    def hx(d):
-        return rcopy(hs_buf.at[d], hr_buf.at[d], hx_s.at[d], hx_r.at[d], dev(z, x, y, 1 - c))
-
-    def head_other(d):
-        head_product(mod(y + d, NY), 1 - c, hs_buf.at[d])
-        hx(d).start()
-
-    fori(0, NY, head_other)
-    fori(0, NY, lambda d: head_product(mod(y + d, NY), c, ho_buf.at[d]))
-
-    def hm(d, xx):
+    h_buf[...] = jnp.zeros_like(h_buf)
+
+    def head_product(e, i):
+        p = lax.dot_general(dmat[...], wbuf[mod(zg + e, NY) * 4 + i], NT, preferred_element_type=F32)
+        half = pl.ds(pl.multiple_of(lax.rem(i, 2) * 32, 32), 32)
+        for xx in range(NX):
+            h_buf[e, lax.div(i, 2), xx, half, 0:WC] = p[xx * 32 : xx * 32 + 32]
+
+    def hx(e):
+        return rcopy(h_buf.at[e, 1 - c], hr_buf.at[e], hx_s.at[e], hx_r.at[e], dev(z, x, y, 1 - c))
+
+    def head_group(e):
+        fori(0, 4, lambda i: head_product(e, i))
+        hx(e).start()
+
+    def hm(e, xx):
         return rcopy(
-            hmsg.at[d, xx],
+            hmsg.at[e, xx],
             hrb.at[x * 4 + y],
-            hm_s.at[d * 4 + xx],
+            hm_s.at[e * 4 + xx],
             hm_r.at[x * 4 + y],
-            dev(z, xx, mod(y + d, NY), c),
+            dev(z, xx, mod(zg + e, NY), c),
         )
+
+    def away_head(fn):
+        def each(e, xx):
+            @pl.when((mod(zg + e, NY) != y) | (xx != x))
+            def _():
+                fn(e, xx)
+
+        return lambda i: each(lax.div(i, 4), lax.rem(i, 4))
+
+    def head_send(e):
+        hx(e).wait_recv()
+        hmsg[e] = (h_buf[e, c] + hr_buf[e]).astype(BF16)
+        fori(e * 4, e * 4 + 4, away_head(lambda e, xx: hm(e, xx).start()))
+
+    def head_step(i):
+        @pl.when(i == 3)
+        def _():
+            w_forward(8)
+
+        head_group(i + lax.div(i, 2) - 2 * lax.div(i, 3))
+
+    fori(0, 4, head_step)
+    fori(0, 4, lambda i: head_send(i + lax.div(i, 2) - 2 * lax.div(i, 3)))
+    hrb[x * 4 + y] = hmsg[mod(y - zg, NY), x]
 
     def away(fn):
         def each(d, xx):
@@ -404,25 +469,16 @@
 
         return lambda i: each(lax.div(i, 4), lax.rem(i, 4))
 
-    def head_send(i):
-        d = lax.rem(i + 1, NY)
-        hx(d).wait_recv()
-        hmsg[d] = (ho_buf[d] + hr_buf[d]).astype(BF16)
-        fori(d * 4, d * 4 + 4, away(lambda d, xx: hm(d, xx).start()))
-
-    fori(0, NY, head_send)
-    hrb[x * 4 + y] = hmsg[0, x]
-
-    def product(g, cc, main):
+    half_other = pl.ds(pl.multiple_of((1 - c) * 160, 8), 160)
+    half_mine = pl.ds(pl.multiple_of(c * 160, 8), 160)
+
+    def cm(d):
+        return rcopy(cs_main.at[d, half_other], cr_main.at[d], cm_s.at[d], cm_r.at[d], dev(z, x, y, 1 - c))
+
+    def make(d):
         a = abuf[...].reshape(4 * 128, KW)
-        wt = wbuf[pl.ds(g * 4 + cc * 2, 2)].reshape(2 * WC, KW)
-        main[...] = lax.dot_general(wt, a, NT, preferred_element_type=F32)
-
-    def cm(d):
-        return rcopy(cs_main.at[d], cr_main.at[d], cm_s.at[d], cm_r.at[d], dev(z, x, y, 1 - c))
-
-    def make(d):
-        product(mod(y + d, NY), 1 - c, cs_main.at[d])
+        wt = wbuf[pl.ds(mod(y + d, NY) * 4, 4)].reshape(4 * WC, KW)
+        cs_main[d] = lax.dot_general(wt, a, NT, preferred_element_type=F32)
         cm(d).start()
 
     fori(0, NY, make)
@@ -431,6 +487,8 @@
         src = lax.rem(x * 4 + y + p, 16)
         return rcopy(hmsg.at[0, 0], hrb.at[src], hm_s.at[0], hm_r.at[src], dev(z, x, y, 1 - c))
 
+    gain_in.wait()
+    gain2[...] = gain_ref[...].astype(F32).reshape(1, 5120)
     fori(1, 16, lambda p: hm_in(p).wait_recv())
     hlane = lax.broadcasted_iota(jnp.int32, (32, HD), 1)
     hproj = jnp.zeros((32, KW), F32)
@@ -461,6 +519,9 @@
         ref = hrows(lax.div(i, 4), lax.rem(i, 4) * NC + cc)
         return rcopy(ref, ref, hc_s.at[p], hc_r.at[p], dev(z, x, y, 1 - c))
 
+    def from_(p):
+        return lax.rem(x * 4 + y - p + 16, 16)
+
     def dbc(d, yy):
         ref = drows(yy * NC + c)
         return rcopy(ref, ref, db_s.at[d], db_r.at[d], dev(z, x, mod(y + d, NY), c))
@@ -469,28 +530,18 @@
         ref = drows(yy * NC + cc)
         return rcopy(ref, ref, dc_s.at[d], dc_r.at[d], dev(z, x, y, 1 - c))
 
-    fori(1, 16, lambda p: hbc(p, x * 4 + y).start())
-    hcc(0, x * 4 + y, c).start()
+    fori(1, 16, lambda p: hbc(p, from_(0)).start())
+    hcc(0, from_(0), c).start()
+    dhid_in.wait()
     dres = (dhid_ref[...].astype(F32) + hproj[16:20]).astype(BF16)
     dout_ref[...] = dres
     drows(t)[...] = jnp.concatenate([dres.astype(F32), jnp.zeros((12, KW), F32)], axis=0).astype(BF16)
     fori(1, NY, lambda d: dbc(d, y).start())
     dcc(0, y, c).start()
 
-    fori(0, NY, lambda d: product(mod(y + d, NY), c, co_main.at[d]))
-
-    def finish(d):
-        cm(d).wait_recv()
-        for xx in range(NX):
-            ls = slice(xx * 128, (xx + 1) * 128)
-            msg[d * 4 + xx] = (co_main[d, :, ls] + cr_main[d, :, ls]).astype(BF16)
-
-    fori(0, NY, finish)
-
     def hfwd(p):
-        i = lax.rem(x * 4 + y - p + 16, 16)
-        hbc(p, i).wait_recv()
-        hcc(p, i, c).start()
+        hbc(p, from_(p)).wait_recv()
+        hcc(p, from_(p), c).start()
 
     fori(1, 16, hfwd)
 
@@ -500,6 +551,55 @@
         dcc(d, yy, c).start()
 
     fori(1, NY, dfwd)
+
+    fori(0, NY, lambda d: dcc(d, mod(y - d, NY), 1 - c).wait_recv())
+    fori(0, 16, lambda p: hcc(p, from_(p), 1 - c).wait_recv())
+    hw_copy.wait()
+
+    def chunk(i):
+        return pl.ds(pl.multiple_of(i * KW, HD), KW)
+
+    def square(i, acc):
+        v = hbuf[:, chunk(i)].astype(F32)
+        return acc + jnp.sum(v * v, axis=-1, keepdims=True)
+
+    ssq = lax.fori_loop(0, 8, square, jnp.zeros((80, 1), F32))
+    inv = lax.rsqrt(ssq / 5120.0 + EPS)
+    vocab = hwbuf.shape[0]
+
+    def logit(i, acc):
+        v = hbuf[:, chunk(i)].astype(F32)
+        n = (v * inv * gain2[:, chunk(i)]).astype(BF16)
+        return acc + lax.dot_general(n, hwbuf[:, chunk(i)], NT, preferred_element_type=F32)
+
+    logits = lax.fori_loop(0, 8, logit, jnp.zeros((80, vocab), F32))
+    lm = jnp.max(logits, axis=-1, keepdims=True)
+    ll = jnp.sum(jnp.exp(logits - lm), axis=-1, keepdims=True)
+
+    ln = lax.broadcasted_iota(jnp.int32, (80, HD), 1)
+    tmat[...] = jnp.zeros_like(tmat)
+    tmat[0:80, :] = jnp.where(ln == 0, lm, jnp.where(ln == 1, ll, 0.0))
+    me = x * 8 + t
+    lsz[z] = tmat[...].T[0:8, :]
+
+    def lzc(d, i):
+        return rcopy(lsz.at[i], lsz.at[i], lz_s.at[d], lz_r.at[d], dev(mod(z + d, NZ), x, y, c))
+
+    def lsc(p, i):
+        return rcopy(lst.at[i], lst.at[i], ls_s.at[p], ls_r.at[p], plane(p))
+
+    def join(ref, n):
+        f = ref.reshape(n * 8, HD)
+        ms = f[pl.ds(0, n, stride=8), :]
+        lls = f[pl.ds(1, n, stride=8), :]
+        top = jnp.max(ms, axis=0, keepdims=True)
+        return top, jnp.sum(lls * jnp.exp(ms - top), axis=0, keepdims=True)
+
+    def far(n):
+        k = lax.div(n + 1, 2)
+        return 8 + k - 2 * k * lax.rem(n, 2)
+
+    fori(0, NZ - 1, lambda n: lzc(far(n), z).start())
 
     def r_copy(d, xx):
         return rcopy(
@@ -510,52 +610,23 @@
             dev(z, xx, mod(y + d, NY), c),
         )
 
+    def finish(d):
+        cm(d).wait_recv()
+        own = cs_main.at[d, half_mine]
+        for xx in range(NX):
+            ls = slice(xx * 128, (xx + 1) * 128)
+            msg[d * 4 + xx] = (own[:, ls] + cr_main[d, :, ls]).astype(BF16)
+
+    fori(0, NY, finish)
+
     fori(4, 20, lambda i: away(lambda d, xx: r_copy(d, xx).start())(lax.rem(i, 16)))
     rbuf[x * 4 + y] = msg[x]
-    fori(0, NY, lambda d: dcc(d, mod(y - d, NY), 1 - c).wait_recv())
-    fori(0, 16, lambda p: hcc(p, lax.rem(x * 4 + y - p + 16, 16), 1 - c).wait_recv())
-    hw_copy.wait()
-
-    def chunk(i):
-        return pl.ds(pl.multiple_of(i * KW, HD), KW)
-
-    def square(i, acc):
-        v = hbuf[:, chunk(i)].astype(F32)
-        return acc + jnp.sum(v * v, axis=-1, keepdims=True)
-
-    ssq = lax.fori_loop(0, 8, square, jnp.zeros((80, 1), F32))
-    inv = lax.rsqrt(ssq / 5120.0 + EPS)
-    vocab = hwbuf.shape[0]
-
-    def logit(i, acc):
-        v = hbuf[:, chunk(i)].astype(F32)
-        n = (v * inv * gain_ref[:, chunk(i)].astype(F32)).astype(BF16)
-        return acc + lax.dot_general(n, hwbuf[:, chunk(i)], NT, preferred_element_type=F32)
-
-    logits = lax.fori_loop(0, 8, logit, jnp.zeros((80, vocab), F32))
-    lm = jnp.max(logits, axis=-1, keepdims=True)
-    ll = jnp.sum(jnp.exp(logits - lm), axis=-1, keepdims=True)
-
-    ln = lax.broadcasted_iota(jnp.int32, (80, HD), 1)
-    tmat[...] = jnp.zeros_like(tmat)
-    tmat[0:80, :] = jnp.where(ln == 0, lm, jnp.where(ln == 1, ll, 0.0))
-    me = x * 8 + t
-    lsz[z] = tmat[...].T[0:8, :]
-
-    def lzc(d, i):
-        return rcopy(lsz.at[i], lsz.at[i], lz_s.at[d], lz_r.at[d], dev(mod(z + d, NZ), x, y, c))
-
-    def lsc(p, i):
-        return rcopy(lst.at[i], lst.at[i], ls_s.at[p], ls_r.at[p], plane(p))
-
-    def join(ref, n):
-        f = ref.reshape(n * 8, HD)
-        ms = f[pl.ds(0, n, stride=8), :]
-        lls = f[pl.ds(1, n, stride=8), :]
-        top = jnp.max(ms, axis=0, keepdims=True)
-        return top, jnp.sum(lls * jnp.exp(ms - top), axis=0, keepdims=True)
-
-    fori(1, NZ, lambda d: lzc(d, z).start())
+
+    fori(1, NZ, lambda d: lzc(d, mod(z - d, NZ)).wait_recv())
+    top, tot = join(lsz, NZ)
+    r8 = lax.broadcasted_iota(jnp.int32, (8, HD), 0)
+    lst[me] = jnp.where(r8 == 0, top, tot)
+    fori(1, 32, lambda p: lsc(p, me).start())
 
     def r_in(p):
         src = lax.rem(x * 4 + y + p, 16)
@@ -573,29 +644,29 @@
         ls = slice(h * HD, (h + 1) * HD)
         out_ref[:, ls] = (hid_ref[:, ls].astype(F32) + big[ls, :].T).astype(BF16)
 
-    fori(1, NZ, lambda d: lzc(d, mod(z - d, NZ)).wait_recv())
-    top, tot = join(lsz, NZ)
-    r8 = lax.broadcasted_iota(jnp.int32, (8, HD), 0)
-    lst[me] = jnp.where(r8 == 0, top, tot)
-    fori(1, 32, lambda p: lsc(p, me).start())
     fori(1, 32, lambda p: lsc(p, lax.rem(me - p + 32, 32)).wait_recv())
     top, tot = join(lst, 32)
     tmat[...] = jnp.broadcast_to(top + jnp.log(tot), (HD, HD))
     lse = tmat[...].T[0:80, 0:1]
     lp = logits - lse
     lp_ref[0:4, :] = lp[64:68]
-    for i in range(64):
-        xx, zz = i // 16, i % 16
-        lp_ref[4 + zz * 4 + xx : 5 + zz * 4 + xx, :] = lp[i : i + 1]
-
-    def ring(i):
-        w_right(lax.div(i, NCH), lax.rem(i, NCH)).wait_send()
-
-        @pl.when(i < 8 * NCH)
-        def _():
-            w_left(lax.div(i, NCH), lax.rem(i, NCH)).wait_send()
-
-    fori(NCH, 9 * NCH, ring)
+    for i in range(lpad.shape[0]):
+        w = min(HD, vocab - i * HD)
+        lpad[i, :, 0:w] = lp[:, i * HD : i * HD + w]
+    for i in range(lpad.shape[0]):
+        w = min(HD, vocab - i * HD)
+        for zz in range(NZ):
+            part = lpad.at[i][pl.ds(zz, 4, stride=16), :]
+            lp_ref[4 + zz * 4 : 8 + zz * 4, i * HD : i * HD + w] = part[:, 0:w]
+
+    def ring(k):
+        for j in range(NCH):
+            w_right(k, j).wait_send()
+            w_left(k, j).wait_send()
+
+    fori(1, 8, ring)
+    for j in range(NCH):
+        (w_right if j < 3 else w_left)(8, j).wait_send()
 
     def three(d):
         dx(d).wait_send()
@@ -615,19 +686,16 @@
 
     fori(0, 4, four)
 
-    def leave(d, xx):
-        hm(d, xx).wait_send()
-        r_copy(d, xx).wait_send()
-
-    fori(0, 16, away(leave))
+    fori(0, 16, away_head(lambda e, xx: hm(e, xx).wait_send()))
+    fori(0, 16, away(lambda d, xx: r_copy(d, xx).wait_send()))
 
     def fifteen(d):
         gz(d, z).wait_send()
-        hbc(d, x * 4 + y).wait_send()
         lzc(d, z).wait_send()
 
     fori(1, 16, fifteen)
-    fori(0, 16, lambda p: hcc(p, lax.rem(x * 4 + y - p + 16, 16), c).wait_send())
+    fori(1, 16, lambda p: hbc(p, from_(0)).wait_send())
+    fori(0, 16, lambda p: hcc(p, from_(p), c).wait_send())
     fori(1, 32, lambda p: lsc(p, me).wait_send())
 
 
@@ -649,11 +717,10 @@
 ):
     vocab = head_weight.shape[1]
     vm = pl.BlockSpec(memory_space=pltpu.VMEM)
-    sm = pl.BlockSpec(memory_space=pltpu.SMEM)
-    hbm = pl.BlockSpec(memory_space=pl.ANY)
+    hbm = pl.BlockSpec(memory_space=pltpu.HBM)
     dma = lambda n: pltpu.SemaphoreType.DMA((n,))
     sems = []
-    for n in (9 * NCH, 8 * NCH, 4, 4, 4, 4, 4, 4, 4, 16, 4, 16, 16, 16, 16, 4, 4, 32, 16):
+    for n in (9 * NCH, 9 * NCH, 4, 4, 4, 4, 4, 4, 4, 16, 4, 16, 16, 16, 16, 4, 4, 32, 16):
         sems += [dma(n), dma(n)]
     return pl.pallas_call(
         kernel,
@@ -662,7 +729,7 @@
             jax.ShapeDtypeStruct((4, KW), BF16),
             jax.ShapeDtypeStruct((68, vocab), F32),
         ),
-        in_specs=[sm, sm, sm, vm, hbm, vm, hbm, vm, vm, vm, hbm, hbm, vm, hbm],
+        in_specs=[hbm] * 14,
         out_specs=(vm, vm, vm),
         scratch_shapes=[
             pltpu.VMEM(head_weight.shape[::-1], BF16),
@@ -679,13 +746,11 @@
             pltpu.VMEM((16, HD), F32),
             pltpu.VMEM((NZ * 16, HD), F32),
             pltpu.VMEM((16, KW), F32),
-            pltpu.VMEM((NY, NX, 64, HD), F32),
-            pltpu.VMEM((NY, NX, 64, HD), F32),
+            pltpu.VMEM((NY, 2, NX, 64, HD), F32),
             pltpu.VMEM((NY, NX, 64, HD), F32),
             pltpu.VMEM((NY, NX, 64, HD), BF16),
             pltpu.VMEM((16, 64, HD), BF16),
-            pltpu.VMEM((4, 160, 512), F32),
-            pltpu.VMEM((4, 160, 512), F32),
+            pltpu.VMEM((4, 320, 512), F32),
             pltpu.VMEM((4, 160, 512), F32),
             pltpu.VMEM((16, 160, HD), BF16),
             pltpu.VMEM((16, 160, HD), BF16),
@@ -695,31 +760,46 @@
             pltpu.VMEM((HD, HD), F32),
             pltpu.VMEM((32, 8, HD), F32),
             pltpu.VMEM((NZ, 8, HD), F32),
+            pltpu.VMEM((-(-vocab // HD), 80, HD), F32),
             pltpu.VMEM((128, KW), BF16),
             pltpu.VMEM((2, 1, 768, HD), BF16),
             pltpu.VMEM((2, 5, 128, HD), BF16),
-            pltpu.SemaphoreType.DMA,
-            dma(4),
+            pltpu.SMEM((64,), jnp.int32),
+            pltpu.SMEM((4,), jnp.int32),
+            pltpu.SMEM((4,), jnp.int32),
+            pltpu.VMEM((128, KW), BF16),
+            pltpu.VMEM((2, 128, HD), BF16),
+            pltpu.VMEM((4, KW), BF16),
+            pltpu.VMEM((4, KW), BF16),
+            pltpu.VMEM((2, 4, HD), BF16),
+            pltpu.VMEM((5120,), BF16),
+            pltpu.VMEM((1, 5120), F32),
+            dma(14),
             *sems,
         ],
         compiler_params=pltpu.CompilerParams(
-            collective_id=0, has_side_effects=True, vmem_limit_bytes=60 * 1024 * 1024
+            collective_id=0, has_side_effects=True, vmem_limit_bytes=48 * 1024 * 1024
         ),
     )(
-        prefix_lengths,
-        cache_lengths,
-        slot_table,
-        prefill_hidden,
-        prefill_query_rows,
-        prefill_key_value,
-        request_prefix_cache,
-        decode_hidden,
-        decode_query_rows,
-        decode_kv,
-        decode_slot_cache,
-        out_weight.T,
-        final_gain.reshape(1, -1),
-        head_weight.T,
+        *[
+            pltpu.with_memory_space_constraint(a, pltpu.HBM)
+            for a in (
+                prefix_lengths,
+                cache_lengths,
+                slot_table,
+                prefill_hidden,
+                prefill_query_rows,
+                prefill_key_value,
+                request_prefix_cache,
+                decode_hidden,
+                decode_query_rows,
+                decode_kv,
+                decode_slot_cache,
+                out_weight.T,
+                final_gain,
+                head_weight.T,
+            )
+        ]
     )
 
 

time: 92.5 us -> 87.1 us (0.942)
  local copies, waits for them, and re-layouts: 5.75 us -> 1.91 us
  Pallas kernels: 85.8 us -> 84.5 us
    unnamed x3, local copies, waits for them, and re-layouts: 4.43 us -> 1.91 us
    pallas_call x1, Pallas kernels: 85.8 us -> 84.5 us  [local(): pl.pallas_call(kernel, out_shape=(jax.ShapeDtypeStruct((128, KW), BF16),...]
    reshape x1 -> x0, local copies, waits for them, and re-layouts: 1.32 us -> none  [local(): final_gain.reshape(1, -1)]
where the time goes in v3:
time: 87.1 us; the launch traced here: 87 us
  Pallas kernels  84.5 us (97%)
  local copies, waits for them, and re-layouts  1.91 us (2%)
    pallas_call x1, Pallas kernels, local(): pl.pallas_call(kernel, out_shape=(jax.ShapeDtypeStruct((128, KW), BF16),...  84.5 us
    unnamed x3, local copies, waits for them, and re-layouts  1.91 us

profile of v3, /device:TPU:1, one launch (start us, length us, event | category | flops | bytes accessed | tf_op | source)
XLA Modules:
  0.0 87.0 jit_solution(2548242451543910059)
XLA Ops:
  0.6 84.5 %shard_map.157 = (bf16[128,640]{1,0:T(8,128)(2,1)S(1)}, bf16[4,640]{1,0:T(4,128)(2,1)S(1)}, f32[68,297]{1,0:T(8,128)S(1)}) custom-call(s32[64]{0:T(128)} %prefix_len_hbm.1, s32[4]{0:T(128)} %cache_len_hbm.1, s32[4]{0:T(128)} %slot_hbm.1, bf16[128,640]{1,0:T(8,128)(2,1)} %hid_hbm.1, bf16[128,640]{1,0:T(8,128)(2,1)} %q_hbm.1, bf16[2,128,128]{2,1,0:T(8,128)(2,1)} %kv_hbm.1, ...), custom_call_target="tpu_custom_call" | custom-call | tf_op jit(solution)/shard_map/pallas_call | solution.py:725
  85.1 0.7 copy.20
  85.8 0.6 copy.21
  86.4 0.6 copy.22

commit v4 on v3

--- a/solution.py
+++ b/solution.py
@@ -80,6 +80,7 @@
     hbuf,
     tmat,
     lst,
+    lsp,
     lsz,
     lpad,
     qv,
@@ -132,6 +133,8 @@
     dc_r,
     ls_s,
     ls_r,
+    lp_s,
+    lp_r,
     lz_s,
     lz_r,
 ):
@@ -149,27 +152,30 @@
             src_ref=src, dst_ref=dst, send_sem=ss, recv_sem=rs, device_id=device, device_id_type=MESH
         )
 
-    barrier = pltpu.get_barrier_semaphore()
-
-    def plane(p):
-        q = lax.rem(x * 8 + t + p, 32)
-        return (z * NX + lax.div(q, 8), lax.rem(q, 8))
-
-    def sig_z(d):
-        pl.semaphore_signal(barrier, inc=1, device_id=dev(mod(z + d, NZ), x, y, c), device_id_type=MESH)
-
-    def sig_p(p):
-        pl.semaphore_signal(barrier, inc=1, device_id=plane(p), device_id_type=MESH)
-
-    fori(1, NZ, sig_z)
-    fori(1, 32, sig_p)
-
     def bring(i, src, dst):
         copy = pltpu.make_async_copy(src, dst, in_sem.at[i])
         copy.start()
         return copy
 
     w_in = bring(0, w_hbm, wbuf.at[z])
+
+    def far(n):
+        k = lax.div(n + 1, 2)
+        return 8 + k - 2 * k * lax.rem(n, 2)
+
+    barrier = pltpu.get_barrier_semaphore()
+
+    def plane(p):
+        q = lax.rem(x * 4 + y + p, 16)
+        return dev(z, lax.div(q, 4), lax.rem(q, 4), c)
+
+    def greet(device):
+        pl.semaphore_signal(barrier, inc=1, device_id=device, device_id_type=MESH)
+
+    fori(0, NZ - 1, lambda n: greet(dev(mod(z + far(n), NZ), x, y, c)))
+    fori(1, 16, lambda p: greet(plane(p)))
+    greet(dev(z, x, y, 1 - c))
+
     dq_in = bring(1, dq_hbm, dq_ref)
     slot_in = bring(2, slot_hbm, slot_ref)
     clen_in = bring(3, cache_len_hbm, cache_len_ref)
@@ -184,7 +190,7 @@
     gain_in = bring(12, gain_hbm, gain_ref)
     hw_copy = bring(13, hw_hbm, hwbuf)
     w_in.wait()
-    pl.semaphore_wait(barrier, NZ - 1 + 31)
+    pl.semaphore_wait(barrier, NZ - 1 + 15 + 1)
 
     def w_right(k, j):
         b = wbuf.at[mod(z - k + 1, NZ), pl.ds(j * WR, WR)]
@@ -356,7 +362,7 @@
         return rcopy(agz.at[slot], agz.at[slot], gz_s.at[d], gz_r.at[d], dev(mod(z + d, NZ), x, y, c))
 
     agz[z] = lrow[...].astype(BF16)
-    fori(1, NZ, lambda d: gz(d, z).start())
+    fori(0, NZ - 1, lambda n: gz(far(n), z).start())
     w_forward(2)
     fori(1, NX, lambda d: a_copy(d, x).start())
     fori(1, 4, lambda d: d1(d, mod(zl - d, 4)).wait_recv())
@@ -579,7 +585,7 @@
     ln = lax.broadcasted_iota(jnp.int32, (80, HD), 1)
     tmat[...] = jnp.zeros_like(tmat)
     tmat[0:80, :] = jnp.where(ln == 0, lm, jnp.where(ln == 1, ll, 0.0))
-    me = x * 8 + t
+    me = x * 4 + y
     lsz[z] = tmat[...].T[0:8, :]
 
     def lzc(d, i):
@@ -594,10 +600,6 @@
         lls = f[pl.ds(1, n, stride=8), :]
         top = jnp.max(ms, axis=0, keepdims=True)
         return top, jnp.sum(lls * jnp.exp(ms - top), axis=0, keepdims=True)
-
-    def far(n):
-        k = lax.div(n + 1, 2)
-        return 8 + k - 2 * k * lax.rem(n, 2)
 
     fori(0, NZ - 1, lambda n: lzc(far(n), z).start())
 
@@ -625,8 +627,16 @@
     fori(1, NZ, lambda d: lzc(d, mod(z - d, NZ)).wait_recv())
     top, tot = join(lsz, NZ)
     r8 = lax.broadcasted_iota(jnp.int32, (8, HD), 0)
+    lsp[c] = jnp.where(r8 == 0, top, tot)
+
+    def lpc(i):
+        return rcopy(lsp.at[i], lsp.at[i], lp_s.at[0], lp_r.at[0], dev(z, x, y, 1 - c))
+
+    lpc(c).start()
+    lpc(1 - c).wait_recv()
+    top, tot = join(lsp, 2)
     lst[me] = jnp.where(r8 == 0, top, tot)
-    fori(1, 32, lambda p: lsc(p, me).start())
+    fori(1, 16, lambda p: lsc(p, me).start())
 
     def r_in(p):
         src = lax.rem(x * 4 + y + p, 16)
@@ -644,8 +654,8 @@
         ls = slice(h * HD, (h + 1) * HD)
         out_ref[:, ls] = (hid_ref[:, ls].astype(F32) + big[ls, :].T).astype(BF16)
 
-    fori(1, 32, lambda p: lsc(p, lax.rem(me - p + 32, 32)).wait_recv())
-    top, tot = join(lst, 32)
+    fori(1, 16, lambda p: lsc(p, from_(p)).wait_recv())
+    top, tot = join(lst, 16)
     tmat[...] = jnp.broadcast_to(top + jnp.log(tot), (HD, HD))
     lse = tmat[...].T[0:80, 0:1]
     lp = logits - lse
@@ -696,7 +706,8 @@
     fori(1, 16, fifteen)
     fori(1, 16, lambda p: hbc(p, from_(0)).wait_send())
     fori(0, 16, lambda p: hcc(p, from_(p), c).wait_send())
-    fori(1, 32, lambda p: lsc(p, me).wait_send())
+    fori(1, 16, lambda p: lsc(p, me).wait_send())
+    lpc(c).wait_send()
 
 
 def local(
@@ -720,7 +731,7 @@
     hbm = pl.BlockSpec(memory_space=pltpu.HBM)
     dma = lambda n: pltpu.SemaphoreType.DMA((n,))
     sems = []
-    for n in (9 * NCH, 9 * NCH, 4, 4, 4, 4, 4, 4, 4, 16, 4, 16, 16, 16, 16, 4, 4, 32, 16):
+    for n in (9 * NCH, 9 * NCH, 4, 4, 4, 4, 4, 4, 4, 16, 4, 16, 16, 16, 16, 4, 4, 16, 1, 16):
         sems += [dma(n), dma(n)]
     return pl.pallas_call(
         kernel,
@@ -758,7 +769,8 @@
             pltpu.VMEM((NZ, 16, HD), BF16),
             pltpu.VMEM((80, 5120), BF16),
             pltpu.VMEM((HD, HD), F32),
-            pltpu.VMEM((32, 8, HD), F32),
+            pltpu.VMEM((16, 8, HD), F32),
+            pltpu.VMEM((2, 8, HD), F32),
             pltpu.VMEM((NZ, 8, HD), F32),
             pltpu.VMEM((-(-vocab // HD), 80, HD), F32),
             pltpu.VMEM((128, KW), BF16),

time: 87.1 us -> 86.5 us (level)
  no operation moved by 1% of the time
where the time goes in v4:
time: 86.5 us; the launch traced here: 86.4 us
  Pallas kernels  83.8 us (97%)
  local copies, waits for them, and re-layouts  1.91 us (2%)
    pallas_call x1, Pallas kernels, local(): pl.pallas_call(kernel, out_shape=(jax.ShapeDtypeStruct((128, KW), BF16),...  83.8 us
    unnamed x3, local copies, waits for them, and re-layouts  1.91 us

profile of v4, /device:TPU:1, one launch (start us, length us, event | category | flops | bytes accessed | tf_op | source)
XLA Modules:
  0.0 86.4 jit_solution(3790013521002067891)
XLA Ops:
  0.6 83.8 %shard_map.157 = (bf16[128,640]{1,0:T(8,128)(2,1)S(1)}, bf16[4,640]{1,0:T(4,128)(2,1)S(1)}, f32[68,297]{1,0:T(8,128)S(1)}) custom-call(s32[64]{0:T(128)} %prefix_len_hbm.1, s32[4]{0:T(128)} %cache_len_hbm.1, s32[4]{0:T(128)} %slot_hbm.1, bf16[128,640]{1,0:T(8,128)(2,1)} %hid_hbm.1, bf16[128,640]{1,0:T(8,128)(2,1)} %q_hbm.1, bf16[2,128,128]{2,1,0:T(8,128)(2,1)} %kv_hbm.1, ...), custom_call_target="tpu_custom_call" | custom-call | tf_op jit(solution)/shard_map/pallas_call | solution.py:736
  84.5 0.7 copy.20
  85.2 0.6 copy.21
  85.7 0.6 copy.22
